TPU v7x, 768 devices: a whole 4x8x12 slice. The times are simulated.
768 devices in a mesh: row: 32 (over y, x), col: 24 (over z, core).
Axes of the slice: x: 4, y: 8, z: 12, core: 2. Of those that a mesh axis runs over, the one named last changes fastest.
Arguments:
- features: float32 [131072, 768], P('row', 'col'), may hold values from -6 to 6
- dest_feat: float32 [1536, 768], P('row', 'col'), may hold values from -6 to 6
- owner: int32 [38400, 1], P('row'), may hold values from 0 to 31; in each aligned block of 1200 rows (0 to 1199, 1200 to 2399, ...) at most 75 rows name the same one
- local_row: int32 [38400], P('row'), may hold values from 0 to 4095
- w_self: float32 [768, 1024], P('col'), may hold values from -0.21875 to 0.21875
- w_neigh: float32 [768, 1024], P('col'), may hold values from -0.4375 to 0.4375
- grad_out: float32 [1536, 1024], P('row'), may hold values from -6 to 6
Outputs:
- hidden: float32 [1536, 1024], P('row')
- grad_self: float32 [768, 1024], P('col')
- grad_neigh: float32 [768, 1024], P('col')
Inputs may be any that keep to these rules, and one draw needn't show every extreme that they name: Among the samples of one index of row, at most 75 have the same owner, and some owner has exactly 75.
All inputs are finite; a program needn't handle non-finite values.
Results may differ from a plain program's by a relative error of at most 0.00008.
Values sent between devices are 32-bit elements; how exact they have to be, the bound alone decides.
No kernel may reach another device: no remote copies, remote signals or barrier semaphores. Data moves between devices by JAX's collectives and lax.ppermute only.
A program may use at most 32 MiB of HBM per device.

v0:
```python
import jax
import jax.numpy as jnp
from jax import lax
from jax.sharding import PartitionSpec as P

FAN = 25
DST_DEV = 48


def gelu_tanh(value):
    return jax.nn.gelu(value, approximate=True)


def activate(pre):
    hidden, back_fn = jax.vjp(gelu_tanh, pre)
    return (hidden, back_fn(jnp.ones_like(pre))[0])


def slot_ranks(owners, owner_count):
    samples = owners.shape[0]
    block = 8 * FAN
    blocks = samples // block
    marks = (owners[:, None] == jnp.arange(owner_count, dtype=jnp.int32)[None, :]).astype(
        jnp.float32
    )
    marks = marks.reshape(blocks, block, owner_count)
    lower = (
        jnp.arange(block, dtype=jnp.int32)[:, None] >= jnp.arange(block, dtype=jnp.int32)[None, :]
    ).astype(jnp.float32)
    within = jnp.einsum("ij,bjo->bio", lower, marks, precision=lax.Precision.HIGHEST)
    totals = within[:, block - 1, :]
    offsets = jnp.cumsum(totals, axis=0) - totals
    counted = within + offsets[:, None, :]
    rank = jnp.sum((counted - 1.0) * marks, axis=2).reshape(samples)
    return rank.astype(jnp.int32)


def body(features, dest_feat, owner, local_row, w_self, w_neigh, grad_out):
    owners = owner[:, 0]
    samples = owners.shape[0]
    width = features.shape[1]
    owner_count = lax.axis_size("row")
    capacity = 2 * samples // owner_count
    rank = slot_ranks(owners, owner_count)
    position = owners * capacity + rank
    send_rows = jnp.zeros((owner_count * capacity,), jnp.int32).at[position].set(local_row)
    send_rows = send_rows.reshape(owner_count, capacity)
    rows = jnp.take(
        features, lax.all_to_all(send_rows, "row", split_axis=0, concat_axis=0, tiled=True), axis=0
    )
    fetched = lax.all_to_all(rows, "row", split_axis=0, concat_axis=0, tiled=True)
    picked = jnp.take(fetched.reshape(owner_count * capacity, width), position, axis=0)
    agg = jnp.sum(picked.reshape(DST_DEV, FAN, width), axis=1) / FAN
    pre_part = jnp.dot(
        dest_feat, w_self, precision=lax.Precision.HIGHEST, preferred_element_type=jnp.float32
    )
    pre_part = pre_part + jnp.dot(
        agg, w_neigh, precision=lax.Precision.HIGHEST, preferred_element_type=jnp.float32
    )
    pre = lax.psum(pre_part, "col")
    hidden, slope = activate(pre)
    dpre = grad_out * slope
    part_self = jnp.dot(
        dest_feat.T, dpre, precision=lax.Precision.HIGHEST, preferred_element_type=jnp.float32
    )
    part_neigh = jnp.dot(
        agg.T, dpre, precision=lax.Precision.HIGHEST, preferred_element_type=jnp.float32
    )
    grad_self, grad_neigh = lax.psum((part_self, part_neigh), "row")
    return (hidden, grad_self, grad_neigh)


def solution(mesh):
    return jax.shard_map(
        body,
        mesh=mesh,
        in_specs=(
            P("row", "col"),
            P("row", "col"),
            P("row", None),
            P("row"),
            P("col", None),
            P("col", None),
            P("row", None),
        ),
        out_specs=(P("row", None), P("col", None), P("col", None)),
        check_vma=False,
    )
```

profile of v0, /device:TPU:2, one launch (start us, length us, event | category | flops | bytes accessed | tf_op | source)
XLA Modules:
  0.0 412.5 jit_solution(12705176961445075166)
XLA Ops:
  7.2 0.0 copy-start
  7.2 0.7 reduce
  7.9 0.1 eq.17
  8.0 0.2 convolution_bitcast_fusion
  8.2 0.2 fusion.20
  8.4 0.1 select_reduce_fusion.1
  8.6 0.1 convert_element_type.18
  8.6 0.7 and_reduce_fusion
  9.4 6.6 %scatter_custom_fusion = s32[2400]{0:T(1024)S(1)} fusion(s32[1200]{0:T(1024)S(1)} %reduce.3, s32[1200]{0:T(1024)} %param.10, s32[]{:T(128)} %constant.28.clone.1), kind=kCustom, calls=%fused_computation.37 | custom fusion | bytes 10112 | tf_op jit(solution)/shard_map/scatter | solution.py:46
  16.0 0.7 all_to_all.13
  16.7 13.0 %all-to-all-start = ((s32[32,1,75]{2,1,0:T(1,128)}), s32[32,1,75]{2,1,0:T(1,128)S(1)}, u32[]{:S(2)}, u32[]{:S(2)}) async-start(s32[32,1,75]{2,1,0:T(1,128)} %all_to_all.13), calls=%async_computation | async-start | bytes 32768 | tf_op jit(solution)/shard_map/all_to_all | solution.py:49
  29.8 1.6 copy.15
  31.4 6.9 %all-to-all-done = s32[32,1,75]{2,1,0:T(1,128)S(1)} async-done(((s32[32,1,75]{2,1,0:T(1,128)}), s32[32,1,75]{2,1,0:T(1,128)S(1)}, u32[]{:S(2)}, u32[]{:S(2)}) %all-to-all-start) | async-done | bytes 9632 | tf_op jit(solution)/shard_map/all_to_all | solution.py:49
  38.3 0.1 reshape.94
  38.5 4.2 %gather_fusion = f32[2400,32]{1,0:T(8,128)S(1)} fusion(f32[4096,32]{1,0:T(8,128)S(1)} %copy.15, s32[3072]{0:T(1024)S(1)} %pad_clamp_fusion), kind=kCustom, calls=%fused_computation | custom fusion | bytes 624000 | tf_op jit(solution)/shard_map/jit(_take)/gather | solution.py:48
  42.7 0.4 copy.16
  43.1 0.8 reshape.93
  44.0 0.0 copy-start.3
  44.0 1.1 copy.17
  45.1 5.0 %all-to-all-start.1 = ((f32[32,75,32]{1,2,0:T(8,128)}), f32[32,75,32]{1,2,0:T(8,128)S(1)}, u32[]{:S(2)}, u32[]{:S(2)}) async-start(f32[32,75,32]{1,2,0:T(8,128)} %copy.17), calls=%async_computation.1 | async-start | bytes 1048576 | tf_op jit(solution)/shard_map/all_to_all | solution.py:51
  50.1 0.0 all-reduce.4.cloned.1.call-start
  50.1 0.1 broadcast_in_dim.30
  50.3 0.0 copy-done
  50.3 0.0 copy-done.3
  50.3 0.4 fusion.21
  50.7 12.3 %all-to-all-done.1 = f32[32,75,32]{1,2,0:T(8,128)S(1)} async-done(((f32[32,75,32]{1,2,0:T(8,128)}), f32[32,75,32]{1,2,0:T(8,128)S(1)}, u32[]{:S(2)}, u32[]{:S(2)}) %all-to-all-start.1) | async-done | bytes 307232 | tf_op jit(solution)/shard_map/all_to_all | solution.py:51
  63.0 0.3 copy.18
  63.3 0.3 reshape.91
  63.6 0.4 copy.19
  64.0 2.5 gather_fusion.1
  66.5 0.0 copy-start.2
  66.5 0.2 copy.20
  66.7 0.0 copy-start.1
  66.7 0.5 gather.12
  67.1 0.3 select_reduce_fusion
  67.4 0.0 copy-done.2
  67.4 1.0 convolution_add_fusion
  68.5 0.0 all-reduce.4.cloned.1.call-update
  68.5 0.0 all-reduce.6.cloned.1.call-start
  68.6 167.0 %all-reduce.4.cloned.1.call-done = f32[48,1024]{1,0:T(8,128)} async-done(((f32[48,1024]{1,0:T(8,128)}), f32[48,1024]{1,0:T(8,128)}) %all-reduce.4.cloned.1.call-update) | async-done | bytes 196624 | tf_op jit(solution)/shard_map/psum | solution.py:60
  235.6 0.0 copy-done.1
  235.6 1.7 fusion.8
  237.3 0.9 fusion.11
  238.2 0.9 convolution_bitcast_fusion.1
  239.2 0.0 all-reduce.6.cloned.1.call-update
  239.2 163.4 %all-reduce.6.cloned.1.call-done = (f32[32,1024]{1,0:T(8,128)}, f32[32,1024]{1,0:T(8,128)}) async-done(((f32[32,1024]{1,0:T(8,128)}, f32[32,1024]{1,0:T(8,128)}), (f32[32,1024]{1,0:T(8,128)}, f32[32,1024]{1,0:T(8,128)})) %all-reduce.6.cloned.1.call-update) | async-done | bytes 262160 | tf_op jit(solution)/shard_map/psum | solution.py:69
  402.5 1.6 copy.24
  404.1 1.6 copy.25
  (7 shorter events, 0.1 us)
Async XLA Ops:
  7.2 43.1 %copy-start = (f32[32,1024]{1,0:T(8,128)S(1)}, f32[32,1024]{1,0:T(8,128)}, u32[]{:S(2)}) copy-start(f32[32,1024]{1,0:T(8,128)} %param.11) | copy-start | bytes 393220
  16.7 21.6 %all-to-all-start = ((s32[32,1,75]{2,1,0:T(1,128)}), s32[32,1,75]{2,1,0:T(1,128)S(1)}, u32[]{:S(2)}, u32[]{:S(2)}) async-start(s32[32,1,75]{2,1,0:T(1,128)} %all_to_all.13), calls=%async_computation | async-start | bytes 32768 | tf_op jit(solution)/shard_map/all_to_all | solution.py:49
  44.0 6.3 %copy-start.3 = (f32[48,32]{0,1:T(8,128)S(1)}, f32[48,32]{0,1:T(8,128)}, u32[]{:S(2)}) copy-start(f32[48,32]{0,1:T(8,128)} %param.8) | copy-start | bytes 18436
  45.1 17.9 %all-to-all-start.1 = ((f32[32,75,32]{1,2,0:T(8,128)}), f32[32,75,32]{1,2,0:T(8,128)S(1)}, u32[]{:S(2)}, u32[]{:S(2)}) async-start(f32[32,75,32]{1,2,0:T(8,128)} %copy.17), calls=%async_computation.1 | async-start | bytes 1048576 | tf_op jit(solution)/shard_map/all_to_all | solution.py:51
  50.1 185.5 %all-reduce.4.cloned.1.call-start = ((), (), s32[]{:S(2)}) async-start(), calls=%async_computation.2 | async-start | bytes 393216 | tf_op jit(solution)/shard_map/psum | solution.py:60
  66.5 1.0 copy-start.2
  66.7 168.9 %copy-start.1 = (f32[48,1024]{1,0:T(8,128)S(1)}, f32[48,1024]{1,0:T(8,128)}, u32[]{:S(2)}) copy-start(f32[48,1024]{1,0:T(8,128)} %param.13) | copy-start | bytes 589828
  68.5 334.0 %all-reduce.6.cloned.1.call-start = ((), (), s32[]{:S(2)}) async-start(), calls=%async_computation.3 | async-start | bytes 524288 | tf_op jit(solution)/shard_map/psum | solution.py:69
Sparse Core Ops, SparseCore 0:
  68.6 166.9 all-reduce.3
  240.1 162.4 all-reduce.5
where the time goes:
time: 413 us
  waiting for transfers between devices  350 us (85%)
  local copies, waits for them, and re-layouts  23.2 us (6%)
  starting transfers between devices  18.1 us (4%)
  between operations  14.2 us (3%)
    psum x1, waiting for transfers between devices, body(): pre = lax.psum(pre_part, 'col')  167 us
    psum x1, waiting for transfers between devices, body(): grad_self, grad_neigh = lax.psum((part_self, part_neigh), 'row')  163 us
    all_to_all x1, starting transfers between devices, body(): lax.all_to_all(send_rows, 'row', split_axis=0, concat_axis=0, tiled=True)  13 us
    all_to_all x1, waiting for transfers between devices, body(): lax.all_to_all(rows, 'row', split_axis=0, concat_axis=0, tiled=True)  12.3 us
  transfers between devices with their start and end apart: 4, of which 4 were waited for; matrix products, arithmetic and copies ran while one was open for 1% of the time, Pallas kernels for 0%

commit v1 on v0

v1 whole, which is shorter than its diff:
```python
import jax
import jax.numpy as jnp
from jax import lax
from jax.sharding import Mesh, PartitionSpec as P

FAN = 25
DST = 48
SLOTS = 128
ROW = ("y", "x")
COL = ("z", "core")
N_ROW = 32
N_Z = 12
HIGH = lax.Precision.HIGH
HIGHEST = lax.Precision.HIGHEST


def gelu_tanh(value):
    return jax.nn.gelu(value, approximate=True)


def activate(pre):
    hidden, back_fn = jax.vjp(gelu_tanh, pre)
    return (hidden, back_fn(jnp.ones_like(pre))[0])


def exchange(value, axis):
    return lax.all_to_all(value, axis, split_axis=0, concat_axis=0, tiled=True)


def slot_ranks(owners, owner_count):
    samples = owners.shape[0]
    block = 8 * FAN
    blocks = samples // block
    marks = (owners[:, None] == jnp.arange(owner_count, dtype=jnp.int32)[None, :]).astype(jnp.float32)
    marks = marks.reshape(blocks, block, owner_count)
    lower = (
        jnp.arange(block, dtype=jnp.int32)[:, None] >= jnp.arange(block, dtype=jnp.int32)[None, :]
    ).astype(jnp.float32)
    within = jnp.einsum("ij,bjo->bio", lower, marks, precision=HIGHEST)
    totals = within[:, block - 1, :]
    offsets = jnp.cumsum(totals, axis=0) - totals
    counted = within + offsets[:, None, :]
    rank = jnp.sum((counted - 1.0) * marks, axis=2).reshape(samples)
    return rank.astype(jnp.int32)


def requests(owners, local_row):
    rank = slot_ranks(owners, N_ROW)
    dest = jnp.arange(owners.shape[0], dtype=jnp.int32) // FAN + 1
    named = (owners[None, :] == jnp.arange(N_ROW, dtype=jnp.int32)[:, None]).astype(jnp.float32)
    slot = (rank[:, None] == jnp.arange(SLOTS, dtype=jnp.int32)[None, :]).astype(jnp.float32)
    both = jnp.stack([local_row, dest]).astype(jnp.float32)
    packed = (named[:, None, :] * both[None, :, :]).reshape(2 * N_ROW, owners.shape[0])
    return jnp.dot(packed, slot, precision=HIGHEST).astype(jnp.int32).reshape(N_ROW, 2, SLOTS)


def body(features, dest_feat, owner, local_row, w_self, w_neigh, grad_out):
    width = features.shape[1]
    hid = w_self.shape[1]
    own = dest_feat.T
    tail = jnp.pad(own, ((0, 0), (0, 128 - DST))).reshape(4, 8, 128).transpose(1, 0, 2).reshape(8, 512)
    tail = jnp.pad(tail, ((0, 0), (0, hid - 512)))
    gathered = lax.all_gather(jnp.concatenate([w_self, w_neigh, tail], axis=0), "z", axis=0, tiled=False)

    asked = exchange(requests(owner[:, 0], local_row), ROW)
    rows = jnp.take(features, asked[:, 0, :75], axis=0)
    placed = (
        asked[:, 1, None, :75] == jnp.arange(1, DST + 1, dtype=jnp.int32)[None, :, None]
    ).astype(jnp.float32)
    part = jnp.einsum("rds,rsf->rfd", placed, rows, precision=HIGH)
    part = exchange(part.reshape(N_ROW, 12, 128), ROW)
    agg = jnp.sum(part, axis=0) / FAN
    others = exchange(jnp.broadcast_to(agg[None], (N_Z, 12, 128)), "z").reshape(N_Z * width, DST)
    agg = agg.reshape(width, DST)

    dests = gathered[:, 64:72, :512].reshape(N_Z, 8, 4, 128).transpose(0, 2, 1, 3).reshape(N_Z * width, 128)[:, :DST]
    pre = lax.dot_general(
        dests, gathered[:, :32].reshape(N_Z * width, hid), (((0,), (0,)), ((), ())), precision=HIGH
    )
    pre = pre + lax.dot_general(
        others, gathered[:, 32:64].reshape(N_Z * width, hid), (((0,), (0,)), ((), ())), precision=HIGH
    )
    pre = jnp.sum(lax.all_gather(pre, "core", axis=0, tiled=False), axis=0)
    hidden, slope = activate(pre)
    dpre = grad_out * slope
    part = jnp.dot(jnp.concatenate([own, agg], axis=0), dpre, precision=HIGH)
    part = part.reshape(4, 16, 8, 128).transpose(0, 2, 1, 3).reshape(N_ROW, 16, 128)
    total = jnp.sum(exchange(part, ROW), axis=0)
    grads = exchange(jnp.broadcast_to(total[None], (N_ROW, 16, 128)), ROW)
    grads = grads.reshape(4, 8, 16, 128).transpose(0, 2, 1, 3).reshape(64, hid)
    return (hidden, grads[:32], grads[32:])


def solution(mesh):
    grid = Mesh(mesh.devices.reshape(8, 4, 12, 2), ("y", "x", "z", "core"))
    return jax.shard_map(
        body,
        mesh=grid,
        in_specs=(P(ROW, COL), P(ROW, COL), P(ROW, None), P(ROW), P(COL, None), P(COL, None), P(ROW, None)),
        out_specs=(P(ROW, None), P(COL, None), P(COL, None)),
        check_vma=False,
    )
```

time: 413 us -> 138 us (0.33)
  the two profiles are of different devices: /device:TPU:2 before, /device:TPU:8 now
where the time goes in v1:
time: 138 us
  blocking collectives  39.4 us (29%)
  waiting for transfers between devices  32.5 us (24%)
  starting transfers between devices  30.2 us (22%)
  between operations  14.3 us (10%)
  local copies, waits for them, and re-layouts  13.7 us (10%)
  other arithmetic  3.86 us (3%)
  matrix products  3.75 us (3%)
    all_to_all x2, blocking collectives, exchange(): return lax.all_to_all(value, axis, split_axis=0, concat_axis=0, tiled=True)  37.3 us
    all_to_all x3, waiting for transfers between devices, exchange(): return lax.all_to_all(value, axis, split_axis=0, concat_axis=0, tiled=True)  30.3 us
    all_to_all x3, starting transfers between devices, exchange(): return lax.all_to_all(value, axis, split_axis=0, concat_axis=0, tiled=True)  30.1 us
    gather x3, local copies, waits for them, and re-layouts, body(): rows = jnp.take(features, asked[:, 0, :75], axis=0)  5.45 us
  transfers between devices with their start and end apart: 4, of which 4 were waited for; matrix products, arithmetic and copies ran while one was open for 9% of the time, Pallas kernels for 0%

profile of v1, /device:TPU:8, one launch (start us, length us, event | category | flops | bytes accessed | tf_op | source)
XLA Modules:
  0.0 137.7 jit_solution(7597029700739550248)
XLA Ops:
  7.2 0.0 all-gather.4.cloned.1.call-start
  7.2 0.7 pad_bitcast_fusion
  7.9 0.0 copy-start
  7.9 1.7 %select_maximum_fusion = f32[72,1024]{1,0:T(8,128)} fusion(f32[8,512]{1,0:T(8,128)S(1)} %pad_bitcast_fusion, f32[32,1024]{1,0:T(8,128)} %param.12, f32[32,1024]{1,0:T(8,128)} %param.11), kind=kLoop, calls=%fused_computation.13 | loop fusion | flops 294912 | bytes 573440 | tf_op jit(solution)/shard_map/concatenate | solution.py:63
  9.7 0.0 all-gather.4.cloned.1.call-update
  9.7 0.7 stack.7
  10.4 0.7 reduce
  11.1 0.1 eq.68
  11.3 0.1 broadcast_multiply_fusion
  11.4 0.2 mul.64
  11.6 0.2 convolution_bitcast_fusion.1
  11.8 0.2 fusion.51
  12.0 0.1 select_reduce_fusion
  12.2 0.1 convert_element_type.39
  12.3 1.1 convolution_convert_fusion
  13.3 13.0 %all-to-all-start = ((s32[32,2,128]{2,1,0:T(2,128)}), s32[32,2,128]{2,1,0:T(2,128)S(1)}, u32[]{:S(2)}, u32[]{:S(2)}) async-start(s32[32,2,128]{2,1,0:T(2,128)} %bitcast.11), calls=%async_computation | async-start | bytes 65536 | tf_op jit(solution)/shard_map/all_to_all | solution.py:27
  26.3 0.0 copy-done
  26.3 0.6 copy.16
  27.0 8.1 %all-to-all-done = s32[32,2,128]{2,1,0:T(2,128)S(1)} async-done(((s32[32,2,128]{2,1,0:T(2,128)}), s32[32,2,128]{2,1,0:T(2,128)S(1)}, u32[]{:S(2)}, u32[]{:S(2)}) %all-to-all-start) | async-done | bytes 32800 | tf_op jit(solution)/shard_map/all_to_all | solution.py:27
  35.1 0.1 reshape.209
  35.3 4.2 %gather_fusion = f32[2400,32]{1,0:T(8,128)S(1)} fusion(f32[4096,32]{1,0:T(8,128)S(1)} %copy.16, s32[3072]{0:T(1024)S(1)} %pad_clamp_fusion), kind=kCustom, calls=%fused_computation | custom fusion | bytes 624000 | tf_op jit(solution)/shard_map/jit(_take)/gather | solution.py:66
  39.5 0.4 copy.17
  39.9 0.8 reshape.208
  40.8 0.7 fusion
  41.5 0.2 reshape.201
  41.7 14.9 %all_to_all.25 = f32[32,12,128]{2,1,0:T(8,128)S(1)} all-to-all(f32[32,12,128]{2,1,0:T(8,128)S(1)} %reshape.201), channel_id=1, replica_groups=mesh['y'=8,'x'=4,'z'=12,'core'=2] {'y','x'}, dimensions={0} | all-to-all | bytes 393216 | tf_op jit(solution)/shard_map/all_to_all | solution.py:27
  56.7 0.7 broadcast_in_dim.16
  57.3 12.5 %all-to-all-start.2 = ((f32[12,12,128]{2,1,0:T(8,128)}), f32[12,12,128]{2,1,0:T(8,128)S(1)}, u32[]{:S(2)}, u32[]{:S(2)}) async-start(f32[12,12,128]{2,1,0:T(8,128)} %broadcast_in_dim.16), calls=%async_computation.2 | async-start | bytes 196608 | tf_op jit(solution)/shard_map/all_to_all | solution.py:27
  69.9 0.1 div.26
  69.9 11.4 %all-to-all-done.2 = f32[12,12,128]{2,1,0:T(8,128)S(1)} async-done(((f32[12,12,128]{2,1,0:T(8,128)}), f32[12,12,128]{2,1,0:T(8,128)S(1)}, u32[]{:S(2)}, u32[]{:S(2)}) %all-to-all-start.2) | async-done | bytes 73760 | tf_op jit(solution)/shard_map/all_to_all | solution.py:27
  81.3 0.1 reshape.202
  81.5 2.2 %all-gather.4.cloned.1.call-done = f32[864,1024]{1,0:T(8,128)} async-done(((f32[72,1024]{1,0:T(8,128)}), f32[864,1024]{1,0:T(8,128)}) %all-gather.4.cloned.1.call-update) | async-done | bytes 3538960 | tf_op jit(solution)/shard_map/all_gather | solution.py:63
  83.6 2.1 %fusion.48 = (f32[12,32,1024]{2,1,0:T(8,128)S(1)}, f32[12,32,1024]{2,1,0:T(8,128)S(1)}) fusion(f32[12,72,1024]{2,1,0:T(8,128)} %bitcast.53), kind=kLoop, calls=%fused_computation.77 | loop fusion | bytes 6291456 | tf_op jit(solution)/shard_map/slice | solution.py:81
  85.7 0.9 slice.46
  86.7 0.7 fusion.16
  87.3 0.0 copy-start.1
  87.4 0.0 copy-start.2
  87.4 0.7 convolution_add_fusion
  88.1 2.1 %all-gather.1 = f32[96,1024]{1,0:T(8,128)S(1)} all-gather(f32[48,1024]{1,0:T(8,128)S(1)} %convolution_add_fusion), channel_id=3, replica_groups=mesh['y'=8,'x'=4,'z'=12,'core'=2] {'core'}, dimensions={0}, use_global_device_ids=true | all-gather | bytes 589824 | tf_op jit(solution)/shard_map/all_gather | solution.py:83
  90.2 0.0 copy-done.1
  90.2 0.0 copy-done.2
  90.2 0.4 convolution_bitcast_fusion
  90.7 22.4 %all_to_all.26 = f32[32,16,128]{2,1,0:T(8,128)S(1)} all-to-all(f32[32,16,128]{2,1,0:T(8,128)S(1)} %bitcast.58), channel_id=1, replica_groups=mesh['y'=8,'x'=4,'z'=12,'core'=2] {'y','x'}, dimensions={0} | all-to-all | bytes 524288 | tf_op jit(solution)/shard_map/all_to_all | solution.py:27
  113.2 0.7 broadcast_in_dim.17
  113.9 4.6 %all-to-all-start.4 = ((f32[32,16,128]{2,1,0:T(8,128)}), f32[32,16,128]{2,1,0:T(8,128)S(1)}, u32[]{:S(2)}, u32[]{:S(2)}) async-start(f32[32,16,128]{2,1,0:T(8,128)} %broadcast_in_dim.17), calls=%async_computation.4 | async-start | bytes 524288 | tf_op jit(solution)/shard_map/all_to_all | solution.py:27
  118.5 0.7 multiply_multiply_fusion.2
  119.2 10.8 %all-to-all-done.4 = f32[32,16,128]{2,1,0:T(8,128)S(1)} async-done(((f32[32,16,128]{2,1,0:T(8,128)}), f32[32,16,128]{2,1,0:T(8,128)S(1)}, u32[]{:S(2)}, u32[]{:S(2)}) %all-to-all-start.4) | async-done | bytes 262176 | tf_op jit(solution)/shard_map/all_to_all | solution.py:27
  130.1 0.7 copy_bitcast_fusion
  (19 shorter events, 0.4 us)
Async XLA Ops:
  7.2 76.5 %all-gather.4.cloned.1.call-start = ((), (), s32[]{:S(2)}) async-start(), calls=%async_computation.5 | async-start | bytes 3833856 | tf_op jit(solution)/shard_map/all_gather | solution.py:63
  7.9 18.4 %copy-start = (f32[4096,32]{0,1:T(8,128)S(1)}, f32[4096,32]{0,1:T(8,128)}, u32[]{:S(2)}) copy-start(f32[4096,32]{0,1:T(8,128)} %param.7) | copy-start | bytes 1572868
  13.3 21.8 %all-to-all-start = ((s32[32,2,128]{2,1,0:T(2,128)}), s32[32,2,128]{2,1,0:T(2,128)S(1)}, u32[]{:S(2)}, u32[]{:S(2)}) async-start(s32[32,2,128]{2,1,0:T(2,128)} %bitcast.11), calls=%async_computation | async-start | bytes 65536 | tf_op jit(solution)/shard_map/all_to_all | solution.py:27
  57.3 24.0 %all-to-all-start.2 = ((f32[12,12,128]{2,1,0:T(8,128)}), f32[12,12,128]{2,1,0:T(8,128)S(1)}, u32[]{:S(2)}, u32[]{:S(2)}) async-start(f32[12,12,128]{2,1,0:T(8,128)} %broadcast_in_dim.16), calls=%async_computation.2 | async-start | bytes 196608 | tf_op jit(solution)/shard_map/all_to_all | solution.py:27
  87.3 2.8 %copy-start.1 = (f32[48,32]{0,1:T(8,128)S(1)}, f32[48,32]{0,1:T(8,128)}, u32[]{:S(2)}) copy-start(f32[48,32]{0,1:T(8,128)} %param.8) | copy-start | bytes 18436
  87.4 2.8 %copy-start.2 = (f32[48,1024]{1,0:T(8,128)S(1)}, f32[48,1024]{1,0:T(8,128)}, u32[]{:S(2)}) copy-start(f32[48,1024]{1,0:T(8,128)} %param.13) | copy-start | bytes 589828
  113.9 16.1 %all-to-all-start.4 = ((f32[32,16,128]{2,1,0:T(8,128)}), f32[32,16,128]{2,1,0:T(8,128)S(1)}, u32[]{:S(2)}, u32[]{:S(2)}) async-start(f32[32,16,128]{2,1,0:T(8,128)} %broadcast_in_dim.17), calls=%async_computation.4 | async-start | bytes 524288 | tf_op jit(solution)/shard_map/all_to_all | solution.py:27
Sparse Core Ops, SparseCore 0:
  10.4 73.1 all-gather.3

commit v2 on v1

--- a/solution.py
+++ b/solution.py
@@ -58,9 +58,7 @@
     width = features.shape[1]
     hid = w_self.shape[1]
     own = dest_feat.T
-    tail = jnp.pad(own, ((0, 0), (0, 128 - DST))).reshape(4, 8, 128).transpose(1, 0, 2).reshape(8, 512)
-    tail = jnp.pad(tail, ((0, 0), (0, hid - 512)))
-    gathered = lax.all_gather(jnp.concatenate([w_self, w_neigh, tail], axis=0), "z", axis=0, tiled=False)
+    weights = lax.all_gather(jnp.concatenate([w_self, w_neigh], axis=0), "z", axis=0, tiled=True)
 
     asked = exchange(requests(owner[:, 0], local_row), ROW)
     rows = jnp.take(features, asked[:, 0, :75], axis=0)
@@ -69,21 +67,15 @@
     ).astype(jnp.float32)
     part = jnp.einsum("rds,rsf->rfd", placed, rows, precision=HIGH)
     part = exchange(part.reshape(N_ROW, 12, 128), ROW)
-    agg = jnp.sum(part, axis=0) / FAN
-    others = exchange(jnp.broadcast_to(agg[None], (N_Z, 12, 128)), "z").reshape(N_Z * width, DST)
-    agg = agg.reshape(width, DST)
-
-    dests = gathered[:, 64:72, :512].reshape(N_Z, 8, 4, 128).transpose(0, 2, 1, 3).reshape(N_Z * width, 128)[:, :DST]
-    pre = lax.dot_general(
-        dests, gathered[:, :32].reshape(N_Z * width, hid), (((0,), (0,)), ((), ())), precision=HIGH
-    )
-    pre = pre + lax.dot_general(
-        others, gathered[:, 32:64].reshape(N_Z * width, hid), (((0,), (0,)), ((), ())), precision=HIGH
-    )
+    agg = (jnp.sum(part, axis=0) / FAN).reshape(width, DST)
+    both = jnp.concatenate([own, agg], axis=0)
+    sent = jnp.broadcast_to(both.reshape(1, 24, 128), (N_Z, 24, 128))
+    others = exchange(sent, "z").reshape(N_Z * 2 * width, DST)
+    pre = lax.dot_general(others, weights, (((0,), (0,)), ((), ())), precision=HIGH)
     pre = jnp.sum(lax.all_gather(pre, "core", axis=0, tiled=False), axis=0)
     hidden, slope = activate(pre)
     dpre = grad_out * slope
-    part = jnp.dot(jnp.concatenate([own, agg], axis=0), dpre, precision=HIGH)
+    part = jnp.dot(both, dpre, precision=HIGH)
     part = part.reshape(4, 16, 8, 128).transpose(0, 2, 1, 3).reshape(N_ROW, 16, 128)
     total = jnp.sum(exchange(part, ROW), axis=0)
     grads = exchange(jnp.broadcast_to(total[None], (N_ROW, 16, 128)), ROW)

time: 138 us -> 137 us (level)
  blocking collectives: 39.4 us -> 64.9 us
  starting transfers between devices: 30.2 us -> 17.6 us
  waiting for transfers between devices: 32.5 us -> 21.2 us
  local copies, waits for them, and re-layouts: 13.7 us -> 9.46 us
  matrix products: 3.75 us -> 5.4 us
    all_to_all x2 -> x3, blocking collectives: 37.3 us -> 62.8 us  [exchange(): return lax.all_to_all(value, axis, split_axis=0, concat_axis=0, tiled=True)]
    all_to_all x3 -> x2, starting transfers between devices: 30.1 us -> 17.6 us  [exchange(): return lax.all_to_all(value, axis, split_axis=0, concat_axis=0, tiled=True)]
    all_to_all x3 -> x2, waiting for transfers between devices: 30.3 us -> 18.9 us  [exchange(): return lax.all_to_all(value, axis, split_axis=0, concat_axis=0, tiled=True)]
    slice x2 -> x0, local copies, waits for them, and re-layouts: 3.05 us -> none  [the longest x1 2.1 us: body(): gathered[:, 32:64].reshape(N_Z * width, hid)]
    dot_general x3 -> x2, matrix products: 1.71 us -> 3.36 us  [the longest x1 2.99 us: body(): lax.dot_general(others, weights, (((0,), (0,)), ((), ())), precision=HIGH)]
  transfers between devices with their start and end apart: 4 -> 3, of which waited for: 4 -> 3; matrix products, arithmetic and copies ran while one was open for 9% -> 9% of each run, Pallas kernels for 0% -> 0%
where the time goes in v2:
time: 137 us
  blocking collectives  64.9 us (47%)
  waiting for transfers between devices  21.2 us (15%)
  starting transfers between devices  17.6 us (13%)
  between operations  14.3 us (10%)
  local copies, waits for them, and re-layouts  9.46 us (7%)
  matrix products  5.4 us (4%)
  other arithmetic  3.87 us (3%)
    all_to_all x3, blocking collectives, exchange(): return lax.all_to_all(value, axis, split_axis=0, concat_axis=0, tiled=True)  62.8 us
    all_to_all x2, waiting for transfers between devices, exchange(): return lax.all_to_all(value, axis, split_axis=0, concat_axis=0, tiled=True)  18.9 us
    all_to_all x2, starting transfers between devices, exchange(): return lax.all_to_all(value, axis, split_axis=0, concat_axis=0, tiled=True)  17.6 us
    gather x3, local copies, waits for them, and re-layouts, body(): rows = jnp.take(features, asked[:, 0, :75], axis=0)  5.45 us
    dot_general x1, matrix products, body(): lax.dot_general(others, weights, (((0,), (0,)), ((), ())), precision=HIGH)  2.99 us
  transfers between devices with their start and end apart: 3, of which 3 were waited for; matrix products, arithmetic and copies ran while one was open for 9% of the time, Pallas kernels for 0%

profile of v2, /device:TPU:8, one launch (start us, length us, event | category | flops | bytes accessed | tf_op | source)
XLA Modules:
  0.0 136.7 jit_solution(16221630335741452678)
XLA Ops:
  7.2 0.0 copy-start
  7.2 0.0 all-gather.3.cloned.1.call-start
  7.2 1.8 %pad_maximum_fusion = f32[64,1024]{1,0:T(8,128)} fusion(f32[32,1024]{1,0:T(8,128)} %param.12, f32[32,1024]{1,0:T(8,128)} %param.11), kind=kLoop, calls=%fused_computation.14 | loop fusion | flops 65536 | bytes 524288 | tf_op jit(solution)/shard_map/concatenate | solution.py:61
  9.0 0.0 all-gather.3.cloned.1.call-update
  9.0 0.7 reduce
  9.7 0.1 eq.68
  9.8 0.2 convolution_bitcast_fusion.1
  10.0 0.2 fusion.44
  10.2 0.1 select_reduce_fusion
  10.3 0.1 convert_element_type.35
  10.4 0.7 stack.7
  11.2 0.1 broadcast_multiply_fusion
  11.3 0.2 mul.64
  11.5 1.1 convolution_convert_fusion
  12.6 13.0 %all-to-all-start = ((s32[32,2,128]{2,1,0:T(2,128)}), s32[32,2,128]{2,1,0:T(2,128)S(1)}, u32[]{:S(2)}, u32[]{:S(2)}) async-start(s32[32,2,128]{2,1,0:T(2,128)} %bitcast.3), calls=%async_computation | async-start | bytes 65536 | tf_op jit(solution)/shard_map/all_to_all | solution.py:27
  25.6 0.0 copy-done
  25.6 0.6 copy.16
  26.3 8.1 %all-to-all-done = s32[32,2,128]{2,1,0:T(2,128)S(1)} async-done(((s32[32,2,128]{2,1,0:T(2,128)}), s32[32,2,128]{2,1,0:T(2,128)S(1)}, u32[]{:S(2)}, u32[]{:S(2)}) %all-to-all-start) | async-done | bytes 32800 | tf_op jit(solution)/shard_map/all_to_all | solution.py:27
  34.4 0.1 reshape.184
  34.5 4.2 %gather_fusion = f32[2400,32]{1,0:T(8,128)S(1)} fusion(f32[4096,32]{1,0:T(8,128)S(1)} %copy.16, s32[3072]{0:T(1024)S(1)} %pad_clamp_fusion), kind=kCustom, calls=%fused_computation | custom fusion | bytes 624000 | tf_op jit(solution)/shard_map/jit(_take)/gather | solution.py:64
  38.8 0.4 copy.17
  39.2 0.0 copy-start.1
  39.2 0.8 reshape.183
  40.1 0.7 fusion
  40.8 0.2 reshape.177
  41.0 14.9 %all_to_all.25 = f32[32,12,128]{2,1,0:T(8,128)S(1)} all-to-all(f32[32,12,128]{2,1,0:T(8,128)S(1)} %reshape.177), channel_id=1, replica_groups=mesh['y'=8,'x'=4,'z'=12,'core'=2] {'y','x'}, dimensions={0} | all-to-all | bytes 393216 | tf_op jit(solution)/shard_map/all_to_all | solution.py:27
  55.9 0.1 div.26
  56.0 0.0 copy-done.1
  56.0 0.1 broadcast_in_dim.18
  56.1 25.1 %all_to_all.26 = f32[12,24,128]{2,1,0:T(8,128)S(1)} all-to-all(f32[12,24,128]{2,1,0:T(8,128)S(1)} %broadcast_in_dim.19), channel_id=1, replica_groups=mesh['y'=8,'x'=4,'z'=12,'core'=2] {'z'}, dimensions={0} | all-to-all | bytes 294912 | tf_op jit(solution)/shard_map/all_to_all | solution.py:27
  81.3 0.2 reshape.178
  81.4 0.0 copy-start.2
  81.5 2.3 %all-gather.3.cloned.1.call-done = f32[768,1024]{1,0:T(8,128)} async-done(((f32[64,1024]{1,0:T(8,128)}), f32[768,1024]{1,0:T(8,128)}) %all-gather.3.cloned.1.call-update) | async-done | bytes 3145744 | tf_op jit(solution)/shard_map/all_gather | solution.py:61
  83.7 3.0 %fusion.45 = f32[48,1024]{1,0:T(8,128)S(1)} fusion(f32[768,48]{1,0:T(8,128)S(1)} %reshape.178, f32[768,1024]{1,0:T(8,128)} %all-gather.3.cloned.1.call-done), kind=kOutput, calls=%fused_computation.72 | convolution fusion | flops 226492416 | bytes 3489792 | tf_op jit(solution)/shard_map/dot_general | solution.py:74
  86.7 2.1 %all-gather = f32[96,1024]{1,0:T(8,128)S(1)} all-gather(f32[48,1024]{1,0:T(8,128)S(1)} %fusion.45), channel_id=2, replica_groups=mesh['y'=8,'x'=4,'z'=12,'core'=2] {'core'}, dimensions={0}, use_global_device_ids=true | all-gather | bytes 589824 | tf_op jit(solution)/shard_map/all_gather | solution.py:75
  88.8 0.0 copy-done.2
  88.8 0.4 convolution_bitcast_fusion
  89.3 22.8 %all_to_all.27 = f32[32,16,128]{2,1,0:T(8,128)S(1)} all-to-all(f32[32,16,128]{2,1,0:T(8,128)S(1)} %bitcast.39), channel_id=1, replica_groups=mesh['y'=8,'x'=4,'z'=12,'core'=2] {'y','x'}, dimensions={0} | all-to-all | bytes 524288 | tf_op jit(solution)/shard_map/all_to_all | solution.py:27
  112.1 0.7 broadcast_in_dim.20
  112.8 4.6 %all-to-all-start.4 = ((f32[32,16,128]{2,1,0:T(8,128)}), f32[32,16,128]{2,1,0:T(8,128)S(1)}, u32[]{:S(2)}, u32[]{:S(2)}) async-start(f32[32,16,128]{2,1,0:T(8,128)} %broadcast_in_dim.20), calls=%async_computation.4 | async-start | bytes 524288 | tf_op jit(solution)/shard_map/all_to_all | solution.py:27
  117.5 0.7 multiply_multiply_fusion.2
  118.2 10.8 %all-to-all-done.4 = f32[32,16,128]{2,1,0:T(8,128)S(1)} async-done(((f32[32,16,128]{2,1,0:T(8,128)}), f32[32,16,128]{2,1,0:T(8,128)S(1)}, u32[]{:S(2)}, u32[]{:S(2)}) %all-to-all-start.4) | async-done | bytes 262176 | tf_op jit(solution)/shard_map/all_to_all | solution.py:27
  129.1 0.7 copy_bitcast_fusion
  (21 shorter events, 0.5 us)
Async XLA Ops:
  7.2 18.5 %copy-start = (f32[4096,32]{0,1:T(8,128)S(1)}, f32[4096,32]{0,1:T(8,128)}, u32[]{:S(2)}) copy-start(f32[4096,32]{0,1:T(8,128)} %param.7) | copy-start | bytes 1572868
  7.2 76.5 %all-gather.3.cloned.1.call-start = ((), (), s32[]{:S(2)}) async-start(), calls=%async_computation.5 | async-start | bytes 3407872 | tf_op jit(solution)/shard_map/all_gather | solution.py:61
  12.6 21.8 %all-to-all-start = ((s32[32,2,128]{2,1,0:T(2,128)}), s32[32,2,128]{2,1,0:T(2,128)S(1)}, u32[]{:S(2)}, u32[]{:S(2)}) async-start(s32[32,2,128]{2,1,0:T(2,128)} %bitcast.3), calls=%async_computation | async-start | bytes 65536 | tf_op jit(solution)/shard_map/all_to_all | solution.py:27
  39.2 16.9 %copy-start.1 = (f32[48,32]{0,1:T(8,128)S(1)}, f32[48,32]{0,1:T(8,128)}, u32[]{:S(2)}) copy-start(f32[48,32]{0,1:T(8,128)} %param.8) | copy-start | bytes 18436
  81.4 7.4 %copy-start.2 = (f32[48,1024]{1,0:T(8,128)S(1)}, f32[48,1024]{1,0:T(8,128)}, u32[]{:S(2)}) copy-start(f32[48,1024]{1,0:T(8,128)} %param.13) | copy-start | bytes 589828
  112.8 16.1 %all-to-all-start.4 = ((f32[32,16,128]{2,1,0:T(8,128)}), f32[32,16,128]{2,1,0:T(8,128)S(1)}, u32[]{:S(2)}, u32[]{:S(2)}) async-start(f32[32,16,128]{2,1,0:T(8,128)} %broadcast_in_dim.20), calls=%async_computation.4 | async-start | bytes 524288 | tf_op jit(solution)/shard_map/all_to_all | solution.py:27
Sparse Core Ops, SparseCore 0:
  10.4 73.2 all-gather.2

commit v3 on v2

--- a/solution.py
+++ b/solution.py
@@ -58,7 +58,6 @@
     width = features.shape[1]
     hid = w_self.shape[1]
     own = dest_feat.T
-    weights = lax.all_gather(jnp.concatenate([w_self, w_neigh], axis=0), "z", axis=0, tiled=True)
 
     asked = exchange(requests(owner[:, 0], local_row), ROW)
     rows = jnp.take(features, asked[:, 0, :75], axis=0)
@@ -69,10 +68,15 @@
     part = exchange(part.reshape(N_ROW, 12, 128), ROW)
     agg = (jnp.sum(part, axis=0) / FAN).reshape(width, DST)
     both = jnp.concatenate([own, agg], axis=0)
-    sent = jnp.broadcast_to(both.reshape(1, 24, 128), (N_Z, 24, 128))
-    others = exchange(sent, "z").reshape(N_Z * 2 * width, DST)
-    pre = lax.dot_general(others, weights, (((0,), (0,)), ((), ())), precision=HIGH)
-    pre = jnp.sum(lax.all_gather(pre, "core", axis=0, tiled=False), axis=0)
+    pre = jnp.dot(dest_feat, w_self, precision=HIGH)
+    pre = pre + lax.dot_general(agg, w_neigh, (((0,), (0,)), ((), ())), precision=HIGH)
+    pair = lax.all_gather(pre.reshape(2, DST // 2, hid), "core", axis=0, tiled=False)
+    half = jnp.sum(lax.dynamic_index_in_dim(pair, lax.axis_index("core"), axis=1, keepdims=False), axis=0)
+    half = half.reshape(3, 8, 4, 256).transpose(0, 2, 1, 3).reshape(N_Z, 8, 256)
+    tile = jnp.sum(exchange(half, "z"), axis=0)
+    half = exchange(jnp.broadcast_to(tile[None], (N_Z, 8, 256)), "z")
+    half = half.reshape(3, 4, 8, 256).transpose(0, 2, 1, 3).reshape(DST // 2, hid)
+    pre = lax.all_gather(half, "core", axis=0, tiled=True)
     hidden, slope = activate(pre)
     dpre = grad_out * slope
     part = jnp.dot(both, dpre, precision=HIGH)

time: 137 us -> 128 us (0.934)
  between operations: 14.3 us -> 0.93 us
  waiting for transfers between devices: 21.2 us -> 29.4 us
  blocking collectives: 64.9 us -> 59.2 us
  starting transfers between devices: 17.6 us -> 22.5 us
  matrix products: 5.4 us -> 2.96 us
  other arithmetic: 3.87 us -> 2.18 us
    all_to_all x2 -> x3, waiting for transfers between devices: 18.9 us -> 29.4 us  [exchange(): return lax.all_to_all(value, axis, split_axis=0, concat_axis=0, tiled=True)]
    all_to_all x3, blocking collectives: 62.8 us -> 55.2 us  [exchange(): return lax.all_to_all(value, axis, split_axis=0, concat_axis=0, tiled=True)]
    all_to_all x2 -> x3, starting transfers between devices: 17.6 us -> 22.5 us  [exchange(): return lax.all_to_all(value, axis, split_axis=0, concat_axis=0, tiled=True)]
    dot_general x1 -> x2, matrix products: 2.99 us -> 0.56 us  [the longest x1 0.28 us: body(): lax.dot_general(agg, w_neigh, (((0,), (0,)), ((), ())), precision=HIGH)]
    all_gather x1 -> x0, waiting for transfers between devices: 2.26 us -> none  [body(): lax.all_gather(jnp.concatenate([w_self, w_neigh], axis=0), 'z', axis=0, t...]
    all_gather x1 -> x2, blocking collectives: 2.09 us -> 4.02 us  [the longest x1 2.09 us: body(): lax.all_gather(pre.reshape(2, DST // 2, hid), 'core', axis=0, tiled=False)]
    concatenate x2 -> x0, other arithmetic: 1.76 us -> none  [the longest x1 1.75 us: body(): jnp.concatenate([w_self, w_neigh], axis=0)]
  transfers between devices with their start and end apart: 3 -> 3, of which waited for: 3 -> 3; matrix products, arithmetic and copies ran while one was open for 9% -> 1% of each run, Pallas kernels for 0% -> 0%
where the time goes in v3:
time: 128 us; the launch traced here: 127 us
  blocking collectives  59.2 us (46%)
  waiting for transfers between devices  29.4 us (23%)
  starting transfers between devices  22.5 us (18%)
  local copies, waits for them, and re-layouts  9.94 us (8%)
  matrix products  2.96 us (2%)
  other arithmetic  2.18 us (2%)
    all_to_all x3, blocking collectives, exchange(): return lax.all_to_all(value, axis, split_axis=0, concat_axis=0, tiled=True)  55.2 us
    all_to_all x3, waiting for transfers between devices, exchange(): return lax.all_to_all(value, axis, split_axis=0, concat_axis=0, tiled=True)  29.4 us
    all_to_all x3, starting transfers between devices, exchange(): return lax.all_to_all(value, axis, split_axis=0, concat_axis=0, tiled=True)  22.5 us
    gather x3, local copies, waits for them, and re-layouts, body(): rows = jnp.take(features, asked[:, 0, :75], axis=0)  5.45 us
  transfers between devices with their start and end apart: 3, of which 3 were waited for; matrix products, arithmetic and copies ran while one was open for 1% of the time, Pallas kernels for 0%

profile of v3, /device:TPU:8, one launch (start us, length us, event | category | flops | bytes accessed | tf_op | source)
XLA Modules:
  0.0 127.1 jit_solution(5020259798126134121)
XLA Ops:
  0.6 0.0 copy-start
  0.6 0.0 copy-start.1
  0.7 0.8 reduce.1
  1.4 0.1 eq.68
  1.5 0.2 convolution_bitcast_fusion.1
  1.7 0.2 fusion.48
  2.0 0.1 select_reduce_fusion
  2.1 0.1 convert_element_type.35
  2.2 0.7 stack.7
  2.9 0.1 broadcast_multiply_fusion
  3.0 0.2 mul.64
  3.3 1.1 convolution_convert_fusion
  4.3 13.0 %all-to-all-start = ((s32[32,2,128]{2,1,0:T(2,128)}), s32[32,2,128]{2,1,0:T(2,128)S(1)}, u32[]{:S(2)}, u32[]{:S(2)}) async-start(s32[32,2,128]{2,1,0:T(2,128)} %bitcast.2), calls=%async_computation | async-start | bytes 65536 | tf_op jit(solution)/shard_map/all_to_all | solution.py:27
  17.3 0.0 copy-done.1
  17.3 0.6 copy.28
  18.0 8.1 %all-to-all-done = s32[32,2,128]{2,1,0:T(2,128)S(1)} async-done(((s32[32,2,128]{2,1,0:T(2,128)}), s32[32,2,128]{2,1,0:T(2,128)S(1)}, u32[]{:S(2)}, u32[]{:S(2)}) %all-to-all-start) | async-done | bytes 32800 | tf_op jit(solution)/shard_map/all_to_all | solution.py:27
  26.1 0.1 reshape.195
  26.3 4.2 %gather_fusion = f32[2400,32]{1,0:T(8,128)S(1)} fusion(f32[4096,32]{1,0:T(8,128)S(1)} %copy.28, s32[3072]{0:T(1024)S(1)} %pad_clamp_fusion), kind=kCustom, calls=%fused_computation | custom fusion | bytes 624000 | tf_op jit(solution)/shard_map/jit(_take)/gather | solution.py:63
  30.5 0.4 copy.29
  30.9 0.8 reshape.194
  31.8 0.0 copy-start.3
  31.8 0.0 copy-start.2
  31.8 0.7 fusion
  32.6 0.9 reshape.185
  33.5 4.9 %all-to-all-start.1 = ((f32[32,12,128]{2,1,0:T(8,128)}), f32[32,12,128]{2,1,0:T(8,128)S(1)}, u32[]{:S(2)}, u32[]{:S(2)}) async-start(f32[32,12,128]{2,1,0:T(8,128)} %reshape.185), calls=%async_computation.1 | async-start | bytes 524288 | tf_op jit(solution)/shard_map/all_to_all | solution.py:27
  38.4 0.0 copy-done
  38.4 0.0 copy-done.3
  38.4 0.3 fusion.49
  38.7 0.0 copy-start.4
  38.7 10.5 %all-to-all-done.1 = f32[32,12,128]{2,1,0:T(8,128)S(1)} async-done(((f32[32,12,128]{2,1,0:T(8,128)}), f32[32,12,128]{2,1,0:T(8,128)S(1)}, u32[]{:S(2)}, u32[]{:S(2)}) %all-to-all-start.1) | async-done | bytes 196640 | tf_op jit(solution)/shard_map/all_to_all | solution.py:27
  49.2 0.1 div.26
  49.3 0.0 copy-done.2
  49.3 0.3 convolution_add_fusion
  49.6 2.1 %all_gather.6 = f32[2,2,24,1024]{3,2,1,0:T(8,128)S(1)} all-gather(f32[1,2,24,1024]{3,2,1,0:T(8,128)S(1)} %bitcast.51), channel_id=1, replica_groups=mesh['y'=8,'x'=4,'z'=12,'core'=2] {'core'}, dimensions={0}, use_global_device_ids=true | all-gather | bytes 589824 | tf_op jit(solution)/shard_map/all_gather | solution.py:73
  51.7 24.0 %all_to_all.30 = f32[12,8,256]{2,1,0:T(8,128)S(1)} all-to-all(f32[12,8,256]{2,1,0:T(8,128)S(1)} %bitcast.54), channel_id=1, replica_groups=mesh['y'=8,'x'=4,'z'=12,'core'=2] {'z'}, dimensions={0} | all-to-all | bytes 196608 | tf_op jit(solution)/shard_map/all_to_all | solution.py:27
  75.8 14.3 %all_to_all.31 = f32[12,8,256]{2,1,0:T(8,128)S(1)} all-to-all(f32[12,8,256]{2,1,0:T(8,128)S(1)} %broadcast_in_dim.16), channel_id=1, replica_groups=mesh['y'=8,'x'=4,'z'=12,'core'=2] {'z'}, dimensions={0} | all-to-all | bytes 196608 | tf_op jit(solution)/shard_map/all_to_all | solution.py:27
  90.0 1.9 %all_gather.7 = f32[48,1024]{1,0:T(8,128)S(1)} all-gather(f32[24,1024]{1,0:T(8,128)S(1)} %bitcast.55), channel_id=1, replica_groups=mesh['y'=8,'x'=4,'z'=12,'core'=2] {'core'}, dimensions={0}, use_global_device_ids=true | all-gather | bytes 294912 | tf_op jit(solution)/shard_map/all_gather | solution.py:79
  92.0 0.0 copy-done.4
  92.0 0.4 convolution_bitcast_fusion
  92.5 16.9 %all_to_all.32 = f32[32,16,128]{2,1,0:T(8,128)S(1)} all-to-all(f32[32,16,128]{2,1,0:T(8,128)S(1)} %bitcast.50), channel_id=1, replica_groups=mesh['y'=8,'x'=4,'z'=12,'core'=2] {'y','x'}, dimensions={0} | all-to-all | bytes 524288 | tf_op jit(solution)/shard_map/all_to_all | solution.py:27
  109.4 0.7 broadcast_in_dim.17
  110.1 4.6 %all-to-all-start.5 = ((f32[32,16,128]{2,1,0:T(8,128)}), f32[32,16,128]{2,1,0:T(8,128)S(1)}, u32[]{:S(2)}, u32[]{:S(2)}) async-start(f32[32,16,128]{2,1,0:T(8,128)} %broadcast_in_dim.17), calls=%async_computation.5 | async-start | bytes 524288 | tf_op jit(solution)/shard_map/all_to_all | solution.py:27
  114.7 0.7 multiply_multiply_fusion.2
  115.5 10.8 %all-to-all-done.5 = f32[32,16,128]{2,1,0:T(8,128)S(1)} async-done(((f32[32,16,128]{2,1,0:T(8,128)}), f32[32,16,128]{2,1,0:T(8,128)S(1)}, u32[]{:S(2)}, u32[]{:S(2)}) %all-to-all-start.5) | async-done | bytes 262176 | tf_op jit(solution)/shard_map/all_to_all | solution.py:27
  126.3 0.7 copy_bitcast_fusion
  (21 shorter events, 0.5 us)
Async XLA Ops:
  0.6 37.7 %copy-start = (f32[32,1024]{1,0:T(8,128)S(1)}, f32[32,1024]{1,0:T(8,128)}, u32[]{:S(2)}) copy-start(f32[32,1024]{1,0:T(8,128)} %param.11) | copy-start | bytes 393220
  0.6 16.7 %copy-start.1 = (f32[4096,32]{0,1:T(8,128)S(1)}, f32[4096,32]{0,1:T(8,128)}, u32[]{:S(2)}) copy-start(f32[4096,32]{0,1:T(8,128)} %param.7) | copy-start | bytes 1572868
  4.3 21.8 %all-to-all-start = ((s32[32,2,128]{2,1,0:T(2,128)}), s32[32,2,128]{2,1,0:T(2,128)S(1)}, u32[]{:S(2)}, u32[]{:S(2)}) async-start(s32[32,2,128]{2,1,0:T(2,128)} %bitcast.2), calls=%async_computation | async-start | bytes 65536 | tf_op jit(solution)/shard_map/all_to_all | solution.py:27
  31.8 6.6 %copy-start.3 = (f32[48,32]{0,1:T(8,128)S(1)}, f32[48,32]{0,1:T(8,128)}, u32[]{:S(2)}) copy-start(f32[48,32]{0,1:T(8,128)} %param.8) | copy-start | bytes 18436
  31.8 17.5 %copy-start.2 = (f32[32,1024]{1,0:T(8,128)S(1)}, f32[32,1024]{1,0:T(8,128)}, u32[]{:S(2)}) copy-start(f32[32,1024]{1,0:T(8,128)} %param.12) | copy-start | bytes 393220
  33.5 15.7 %all-to-all-start.1 = ((f32[32,12,128]{2,1,0:T(8,128)}), f32[32,12,128]{2,1,0:T(8,128)S(1)}, u32[]{:S(2)}, u32[]{:S(2)}) async-start(f32[32,12,128]{2,1,0:T(8,128)} %reshape.185), calls=%async_computation.1 | async-start | bytes 524288 | tf_op jit(solution)/shard_map/all_to_all | solution.py:27
  38.7 53.3 %copy-start.4 = (f32[48,1024]{1,0:T(8,128)S(1)}, f32[48,1024]{1,0:T(8,128)}, u32[]{:S(2)}) copy-start(f32[48,1024]{1,0:T(8,128)} %param.13) | copy-start | bytes 589828
  110.1 16.1 %all-to-all-start.5 = ((f32[32,16,128]{2,1,0:T(8,128)}), f32[32,16,128]{2,1,0:T(8,128)S(1)}, u32[]{:S(2)}, u32[]{:S(2)}) async-start(f32[32,16,128]{2,1,0:T(8,128)} %broadcast_in_dim.17), calls=%async_computation.5 | async-start | bytes 524288 | tf_op jit(solution)/shard_map/all_to_all | solution.py:27

commit v4 on v3

v4 whole, which is shorter than its diff:
```python
import jax
import jax.numpy as jnp
from jax import lax
from jax.experimental import pallas as pl
from jax.experimental.pallas import tpu as pltpu
from jax.sharding import Mesh, PartitionSpec as P

FAN = 25
DST = 48
CAP = 75
ROOM = 80
SLOTS = 128
ROW = ("y", "x")
COL = ("z", "core")
N_ROW = 32
N_Z = 12
HIGH = lax.Precision.HIGH
LANES = (((1,), (1,)), ((), ()))
VMEM = pl.BlockSpec(memory_space=pltpu.VMEM)
SMEM = pl.BlockSpec(memory_space=pltpu.SMEM)
SMALL = pltpu.CompilerParams(vmem_limit_bytes=16 << 20)


def gelu_tanh(value):
    return jax.nn.gelu(value, approximate=True)


def activate(pre):
    hidden, back_fn = jax.vjp(gelu_tanh, pre)
    return (hidden, back_fn(jnp.ones_like(pre))[0])


def exchange(value, axis):
    return lax.all_to_all(value, axis, split_axis=0, concat_axis=0, tiled=True)


def request_kernel(owner_ref, row_ref, out_ref):
    samples = owner_ref.shape[1]
    blocks = -(-samples // 128)
    line = lax.broadcasted_iota(jnp.int32, (2 * N_ROW, 128), 0)
    lane = lax.broadcasted_iota(jnp.int32, (1, 128), 1)
    even = (line & 1) == 0
    before = lax.broadcasted_iota(jnp.int32, (128, 128), 0) >= lax.broadcasted_iota(jnp.int32, (128, 128), 1)
    before = jnp.where(before, 1.0, 0.0).astype(jnp.bfloat16)
    slot = lax.broadcasted_iota(jnp.int32, (SLOTS, 128), 0).astype(jnp.float32)

    def part(ref, block, fill):
        width = min(128, samples - block * 128)
        values = ref[:, block * 128 : block * 128 + width]
        if width < 128:
            values = jnp.concatenate([values, jnp.full((1, 128 - width), fill, jnp.int32)], axis=1)
        return values

    marks, counts = [], []
    for block in range(blocks):
        mark = part(owner_ref, block, -1) == (line >> 1)
        marks.append(mark)
        counts.append(
            lax.dot_general(
                jnp.where(mark, 1.0, 0.0).astype(jnp.bfloat16), before, LANES, preferred_element_type=jnp.float32
            )
        )
    seen = jnp.full((2 * N_ROW, 1), -1.0, jnp.float32)
    lefts, rights = [], []
    for block in range(blocks):
        rows = part(row_ref, block, 0)
        mark, count = marks[block], counts[block]
        rank = jnp.sum(jnp.where(mark & even, count + seen, 0.0), axis=0, keepdims=True)
        seen = seen + count[:, 127:128]
        rights.append(jnp.where(rank == slot, 1.0, 0.0).astype(jnp.bfloat16))
        dest = (lane + block * 128) // FAN + 1
        high = jnp.where(mark, jnp.where(even, rows >> 6, dest), 0).astype(jnp.float32)
        low = jnp.where(mark & even, rows & 63, 0).astype(jnp.float32)
        lefts.append(jnp.concatenate([high, low], axis=0).astype(jnp.bfloat16))
    total = lax.dot_general(
        jnp.concatenate(lefts, axis=1), jnp.concatenate(rights, axis=1), LANES, preferred_element_type=jnp.float32
    )
    first, second = total[: 2 * N_ROW], total[2 * N_ROW :]
    out_ref[...] = (jnp.where(even, first * 64.0, first) + second).astype(jnp.int32)


def requests(owner, local_row):
    return pl.pallas_call(
        request_kernel,
        in_specs=[VMEM, VMEM],
        out_specs=VMEM,
        out_shape=jax.ShapeDtypeStruct((2 * N_ROW, SLOTS), jnp.int32),
        compiler_params=SMALL,
        name="requests",
    )(owner, local_row)


def answer_kernel(index_ref, asked_ref, table_ref, ahead_ref, out_ref, held_ref):
    width = table_ref.shape[1]

    def fetch(r, carry):
        held_ref[r, ROOM - 8 :, :] = jnp.zeros((8, width), jnp.float32)
        for s in range(CAP):
            held_ref[r, s : s + 1, :] = table_ref[pl.ds(index_ref[2 * r, s], 1), :]
        return carry

    lax.fori_loop(0, N_ROW, fetch, 0)
    line = lax.broadcasted_iota(jnp.int32, (DST, ROOM), 0) + 1
    gap = jnp.zeros((16, 128 - 3 * width), jnp.float32)
    for r in range(N_ROW):
        dest = asked_ref[2 * r + 1 : 2 * r + 2, :ROOM]
        place = jnp.where(dest == line, 1.0, 0.0).astype(jnp.bfloat16)
        value = held_ref[r]
        lead = value.astype(jnp.bfloat16)
        rest = (value - lead.astype(jnp.float32)).astype(jnp.bfloat16)
        total = jnp.dot(place, jnp.concatenate([lead, rest], axis=1), preferred_element_type=jnp.float32)
        total = total[:, :width] + total[:, width:]
        out_ref[r] = jnp.concatenate([total[:16], total[16:32], total[32:], gap], axis=1)


def answers(asked, table, ahead):
    width = table.shape[1]
    return pl.pallas_call(
        answer_kernel,
        in_specs=[SMEM, VMEM, VMEM, pl.BlockSpec(memory_space=pl.ANY)],
        out_specs=VMEM,
        out_shape=jax.ShapeDtypeStruct((N_ROW, 16, 128), jnp.float32),
        scratch_shapes=[pltpu.VMEM((N_ROW, ROOM, width), jnp.float32)],
        compiler_params=SMALL,
        name="answers",
    )(asked, asked, table, ahead)


def body(features, dest_feat, owner, local_row, w_self, w_neigh, grad_out):
    width = features.shape[1]
    hid = w_self.shape[1]
    asked = requests(owner.reshape(1, -1), local_row.reshape(1, -1))
    asked = exchange(asked.reshape(N_ROW, 2, SLOTS), ROW).reshape(2 * N_ROW, SLOTS)
    pre_self = jnp.dot(dest_feat, w_self, precision=HIGH)
    part = exchange(answers(asked, features, pre_self), ROW)
    part = jnp.sum(part, axis=0) / FAN
    agg = jnp.concatenate([part[:, k * width : (k + 1) * width] for k in range(DST // 16)], axis=0)
    pre = pre_self + jnp.dot(agg, w_neigh, precision=HIGH)
    pair = lax.all_gather(pre.reshape(2, DST // 2, hid), "core", axis=0, tiled=False)
    half = jnp.sum(lax.dynamic_index_in_dim(pair, lax.axis_index("core"), axis=1, keepdims=False), axis=0)
    half = half.reshape(3, 8, 4, 256).transpose(0, 2, 1, 3).reshape(N_Z, 8, 256)
    tile = jnp.sum(exchange(half, "z"), axis=0)
    half = exchange(jnp.broadcast_to(tile[None], (N_Z, 8, 256)), "z")
    half = half.reshape(3, 4, 8, 256).transpose(0, 2, 1, 3).reshape(DST // 2, hid)
    pre = lax.all_gather(half, "core", axis=0, tiled=True)
    hidden, slope = activate(pre)
    dpre = grad_out * slope
    both = jnp.concatenate([dest_feat.T, agg.T], axis=0)
    part = jnp.dot(both, dpre, precision=HIGH)
    part = part.reshape(4, 16, 8, 128).transpose(0, 2, 1, 3).reshape(N_ROW, 16, 128)
    total = jnp.sum(exchange(part, ROW), axis=0)
    grads = exchange(jnp.broadcast_to(total[None], (N_ROW, 16, 128)), ROW)
    grads = grads.reshape(4, 8, 16, 128).transpose(0, 2, 1, 3).reshape(64, hid)
    return (hidden, grads[:32], grads[32:])


def solution(mesh):
    grid = Mesh(mesh.devices.reshape(8, 4, 12, 2), ("y", "x", "z", "core"))
    return jax.shard_map(
        body,
        mesh=grid,
        in_specs=(P(ROW, COL), P(ROW, COL), P(ROW, None), P(ROW), P(COL, None), P(COL, None), P(ROW, None)),
        out_specs=(P(ROW, None), P(COL, None), P(COL, None)),
        check_vma=False,
    )
```

time: 128 us -> 126 us (0.984)
  blocking collectives: 59.2 us -> 44.9 us
  waiting for transfers between devices: 29.4 us -> 39.1 us
  Pallas kernels: 0 us -> 6.08 us
  local copies, waits for them, and re-layouts: 9.94 us -> 5.55 us
  starting transfers between devices: 22.5 us -> 26.1 us
  matrix products: 2.96 us -> 1.62 us
  other arithmetic: 2.18 us -> 0.85 us
    all_to_all x3 -> x2, blocking collectives: 55.2 us -> 40.9 us  [exchange(): return lax.all_to_all(value, axis, split_axis=0, concat_axis=0, tiled=True)]
    all_to_all x3 -> x4, waiting for transfers between devices: 29.4 us -> 39.1 us  [exchange(): return lax.all_to_all(value, axis, split_axis=0, concat_axis=0, tiled=True)]
    pallas_call x0 -> x2, Pallas kernels: none -> 6.08 us  [the longest x1 4.81 us: answers(): pl.pallas_call(answer_kernel, in_specs=[SMEM, VMEM, VMEM, pl.BlockSpec(me...]
    gather x3 -> x0, local copies, waits for them, and re-layouts: 5.45 us -> none  [body(): rows = jnp.take(features, asked[:, 0, :75], axis=0)]
    all_to_all x3 -> x4, starting transfers between devices: 22.5 us -> 26.1 us  [exchange(): return lax.all_to_all(value, axis, split_axis=0, concat_axis=0, tiled=True)]
    unnamed x12 -> x13, local copies, waits for them, and re-layouts: 0.68 us -> 2.48 us
    dot_general x5 -> x2, matrix products: 2.59 us -> 1.21 us  [the longest x1 1 us: body(): pre_self = jnp.dot(dest_feat, w_self, precision=HIGH)]
  transfers between devices with their start and end apart: 3 -> 4, of which waited for: 3 -> 4; matrix products, arithmetic and copies ran while one was open for 1% -> 3% of each run, Pallas kernels for 0% -> 0%
where the time goes in v4:
time: 126 us; the launch traced here: 125 us
  blocking collectives  44.9 us (36%)
  waiting for transfers between devices  39.1 us (31%)
  starting transfers between devices  26.1 us (21%)
  Pallas kernels  6.08 us (5%)
  local copies, waits for them, and re-layouts  5.55 us (4%)
  matrix products  1.62 us (1%)
    all_to_all x2, blocking collectives, exchange(): return lax.all_to_all(value, axis, split_axis=0, concat_axis=0, tiled=True)  40.9 us
    all_to_all x4, waiting for transfers between devices, exchange(): return lax.all_to_all(value, axis, split_axis=0, concat_axis=0, tiled=True)  39.1 us
    all_to_all x4, starting transfers between devices, exchange(): return lax.all_to_all(value, axis, split_axis=0, concat_axis=0, tiled=True)  26.1 us
    pallas_call x1, Pallas kernels, answers(): pl.pallas_call(answer_kernel, in_specs=[SMEM, VMEM, VMEM, pl.BlockSpec(me...  4.81 us
  transfers between devices with their start and end apart: 4, of which 4 were waited for; matrix products, arithmetic and copies ran while one was open for 3% of the time, Pallas kernels for 0%

profile of v4, /device:TPU:8, one launch (start us, length us, event | category | flops | bytes accessed | tf_op | source)
XLA Modules:
  0.0 125.1 jit_solution(6047424765824760311)
XLA Ops:
  0.6 0.0 copy-start
  0.6 0.7 reshape.45.row_ref
  1.4 0.0 copy-start.1
  1.4 0.7 copy-done.1
  2.1 1.3 %requests.1 = s32[64,128]{1,0:T(8,128)} custom-call(s32[1,1200]{1,0:T(1,128)S(1)} %bitcast.40, s32[1,1200]{1,0:T(1,128)S(1)} %reshape.45.row_ref), custom_call_target="tpu_custom_call" | custom-call | tf_op jit(solution)/shard_map/requests/pallas_call | solution.py:83
  3.3 13.0 %all-to-all-start = ((s32[32,2,128]{2,1,0:T(2,128)}), s32[32,2,128]{2,1,0:T(2,128)S(1)}, u32[]{:S(2)}, u32[]{:S(2)}) async-start(s32[32,2,128]{2,1,0:T(2,128)} %bitcast.1), calls=%async_computation | async-start | bytes 65536 | tf_op jit(solution)/shard_map/all_to_all | solution.py:34
  16.3 0.0 copy-done
  16.3 1.0 fusion.38.ahead_ref
  17.3 1.6 %copy.22.table_ref = f32[4096,32]{1,0:T(8,128)S(1)} copy(f32[4096,32]{0,1:T(8,128)} %param.7) | data formatting | bytes 1048576 | tf_op args[0]
  19.0 0.0 copy-start.2
  19.0 6.1 %all-to-all-done = s32[32,2,128]{2,1,0:T(2,128)S(1)} async-done(((s32[32,2,128]{2,1,0:T(2,128)}), s32[32,2,128]{2,1,0:T(2,128)S(1)}, u32[]{:S(2)}, u32[]{:S(2)}) %all-to-all-start) | async-done | bytes 32800 | tf_op jit(solution)/shard_map/all_to_all | solution.py:34
  25.1 4.8 %answers.1 = f32[32,16,128]{2,1,0:T(8,128)} custom-call(s32[64,128]{1,0:T(8,128)S(1)} %bitcast.38, s32[64,128]{1,0:T(8,128)S(1)} %bitcast.39, f32[4096,32]{1,0:T(8,128)S(1)} %copy.22.table_ref, f32[48,1024]{1,0:T(8,128)S(1)} %fusion.38.ahead_ref), custom_call_target="tpu_custom_call" | custom-call | tf_op jit(solution)/shard_map/answers/pallas_call | solution.py:118
  29.9 0.0 copy-start.3
  29.9 0.0 copy-start.4
  29.9 5.0 %all-to-all-start.1 = ((f32[32,16,128]{2,1,0:T(8,128)}), f32[32,16,128]{2,1,0:T(8,128)S(1)}, u32[]{:S(2)}, u32[]{:S(2)}) async-start(f32[32,16,128]{2,1,0:T(8,128)} %answers.1), calls=%async_computation.1 | async-start | bytes 524288 | tf_op jit(solution)/shard_map/all_to_all | solution.py:34
  34.9 10.8 %all-to-all-done.1 = f32[32,16,128]{2,1,0:T(8,128)S(1)} async-done(((f32[32,16,128]{2,1,0:T(8,128)}), f32[32,16,128]{2,1,0:T(8,128)S(1)}, u32[]{:S(2)}, u32[]{:S(2)}) %all-to-all-start.1) | async-done | bytes 262176 | tf_op jit(solution)/shard_map/all_to_all | solution.py:34
  45.8 0.1 fusion.37
  45.9 0.0 copy-done.2
  45.9 0.2 convolution_add_fusion
  46.1 2.1 %all_gather.6 = f32[2,2,24,1024]{3,2,1,0:T(8,128)S(1)} all-gather(f32[1,2,24,1024]{3,2,1,0:T(8,128)S(1)} %bitcast.44), channel_id=1, replica_groups=mesh['y'=8,'x'=4,'z'=12,'core'=2] {'core'}, dimensions={0}, use_global_device_ids=true | all-gather | bytes 589824 | tf_op jit(solution)/shard_map/all_gather | solution.py:139
  48.2 24.0 %all_to_all.30 = f32[12,8,256]{2,1,0:T(8,128)S(1)} all-to-all(f32[12,8,256]{2,1,0:T(8,128)S(1)} %bitcast.48), channel_id=1, replica_groups=mesh['y'=8,'x'=4,'z'=12,'core'=2] {'z'}, dimensions={0} | all-to-all | bytes 196608 | tf_op jit(solution)/shard_map/all_to_all | solution.py:34
  72.3 0.6 broadcast_in_dim.4
  72.9 3.5 %all-to-all-start.3 = ((f32[12,8,256]{2,1,0:T(8,128)}), f32[12,8,256]{2,1,0:T(8,128)S(1)}, u32[]{:S(2)}, u32[]{:S(2)}) async-start(f32[12,8,256]{2,1,0:T(8,128)} %broadcast_in_dim.4), calls=%async_computation.3 | async-start | bytes 196608 | tf_op jit(solution)/shard_map/all_to_all | solution.py:34
  76.4 0.0 copy-done.3
  76.4 0.1 copy.23
  76.5 11.4 %all-to-all-done.3 = f32[12,8,256]{2,1,0:T(8,128)S(1)} async-done(((f32[12,8,256]{2,1,0:T(8,128)}), f32[12,8,256]{2,1,0:T(8,128)S(1)}, u32[]{:S(2)}, u32[]{:S(2)}) %all-to-all-start.3) | async-done | bytes 98336 | tf_op jit(solution)/shard_map/all_to_all | solution.py:34
  88.0 1.9 %all_gather.7 = f32[48,1024]{1,0:T(8,128)S(1)} all-gather(f32[24,1024]{1,0:T(8,128)S(1)} %bitcast.47), channel_id=1, replica_groups=mesh['y'=8,'x'=4,'z'=12,'core'=2] {'core'}, dimensions={0}, use_global_device_ids=true | all-gather | bytes 294912 | tf_op jit(solution)/shard_map/all_gather | solution.py:145
  89.9 0.0 copy-done.4
  89.9 0.4 convolution_bitcast_fusion
  90.4 16.9 %all_to_all.31 = f32[32,16,128]{2,1,0:T(8,128)S(1)} all-to-all(f32[32,16,128]{2,1,0:T(8,128)S(1)} %bitcast.43), channel_id=1, replica_groups=mesh['y'=8,'x'=4,'z'=12,'core'=2] {'y','x'}, dimensions={0} | all-to-all | bytes 524288 | tf_op jit(solution)/shard_map/all_to_all | solution.py:34
  107.4 0.7 broadcast_in_dim.5
  108.1 4.6 %all-to-all-start.5 = ((f32[32,16,128]{2,1,0:T(8,128)}), f32[32,16,128]{2,1,0:T(8,128)S(1)}, u32[]{:S(2)}, u32[]{:S(2)}) async-start(f32[32,16,128]{2,1,0:T(8,128)} %broadcast_in_dim.5), calls=%async_computation.5 | async-start | bytes 524288 | tf_op jit(solution)/shard_map/all_to_all | solution.py:34
  112.7 0.7 multiply_multiply_fusion.2
  113.4 10.8 %all-to-all-done.5 = f32[32,16,128]{2,1,0:T(8,128)S(1)} async-done(((f32[32,16,128]{2,1,0:T(8,128)}), f32[32,16,128]{2,1,0:T(8,128)S(1)}, u32[]{:S(2)}, u32[]{:S(2)}) %all-to-all-start.5) | async-done | bytes 262176 | tf_op jit(solution)/shard_map/all_to_all | solution.py:34
  124.3 0.7 copy_bitcast_fusion
  (11 shorter events, 0.3 us)
Async XLA Ops:
  0.6 15.7 %copy-start = (f32[32,1024]{1,0:T(8,128)S(1)}, f32[32,1024]{1,0:T(8,128)}, u32[]{:S(2)}) copy-start(f32[32,1024]{1,0:T(8,128)} %param.11) | copy-start | bytes 393220
  1.4 0.7 copy-start.1
  3.3 21.8 %all-to-all-start = ((s32[32,2,128]{2,1,0:T(2,128)}), s32[32,2,128]{2,1,0:T(2,128)S(1)}, u32[]{:S(2)}, u32[]{:S(2)}) async-start(s32[32,2,128]{2,1,0:T(2,128)} %bitcast.1), calls=%async_computation | async-start | bytes 65536 | tf_op jit(solution)/shard_map/all_to_all | solution.py:34
  19.0 26.9 %copy-start.2 = (f32[32,1024]{1,0:T(8,128)S(1)}, f32[32,1024]{1,0:T(8,128)}, u32[]{:S(2)}) copy-start(f32[32,1024]{1,0:T(8,128)} %param.12) | copy-start | bytes 393220
  29.9 46.5 %copy-start.3 = (f32[48,32]{0,1:T(8,128)S(1)}, f32[48,32]{0,1:T(8,128)}, u32[]{:S(2)}) copy-start(f32[48,32]{0,1:T(8,128)} %param.8) | copy-start | bytes 18436
  29.9 60.0 %copy-start.4 = (f32[48,1024]{1,0:T(8,128)S(1)}, f32[48,1024]{1,0:T(8,128)}, u32[]{:S(2)}) copy-start(f32[48,1024]{1,0:T(8,128)} %param.13) | copy-start | bytes 589828
  29.9 15.8 %all-to-all-start.1 = ((f32[32,16,128]{2,1,0:T(8,128)}), f32[32,16,128]{2,1,0:T(8,128)S(1)}, u32[]{:S(2)}, u32[]{:S(2)}) async-start(f32[32,16,128]{2,1,0:T(8,128)} %answers.1), calls=%async_computation.1 | async-start | bytes 524288 | tf_op jit(solution)/shard_map/all_to_all | solution.py:34
  72.9 15.0 %all-to-all-start.3 = ((f32[12,8,256]{2,1,0:T(8,128)}), f32[12,8,256]{2,1,0:T(8,128)S(1)}, u32[]{:S(2)}, u32[]{:S(2)}) async-start(f32[12,8,256]{2,1,0:T(8,128)} %broadcast_in_dim.4), calls=%async_computation.3 | async-start | bytes 196608 | tf_op jit(solution)/shard_map/all_to_all | solution.py:34
  108.1 16.1 %all-to-all-start.5 = ((f32[32,16,128]{2,1,0:T(8,128)}), f32[32,16,128]{2,1,0:T(8,128)S(1)}, u32[]{:S(2)}, u32[]{:S(2)}) async-start(f32[32,16,128]{2,1,0:T(8,128)} %broadcast_in_dim.5), calls=%async_computation.5 | async-start | bytes 524288 | tf_op jit(solution)/shard_map/all_to_all | solution.py:34

commit v5 on v4

--- a/solution.py
+++ b/solution.py
@@ -14,20 +14,14 @@
 COL = ("z", "core")
 N_ROW = 32
 N_Z = 12
+BEND = 0.7978845608
+CUBE = 0.044715
 HIGH = lax.Precision.HIGH
 LANES = (((1,), (1,)), ((), ()))
 VMEM = pl.BlockSpec(memory_space=pltpu.VMEM)
+ANY = pl.BlockSpec(memory_space=pl.ANY)
 SMEM = pl.BlockSpec(memory_space=pltpu.SMEM)
 SMALL = pltpu.CompilerParams(vmem_limit_bytes=16 << 20)
-
-
-def gelu_tanh(value):
-    return jax.nn.gelu(value, approximate=True)
-
-
-def activate(pre):
-    hidden, back_fn = jax.vjp(gelu_tanh, pre)
-    return (hidden, back_fn(jnp.ones_like(pre))[0])
 
 
 def exchange(value, axis):
@@ -90,7 +84,7 @@
     )(owner, local_row)
 
 
-def answer_kernel(index_ref, asked_ref, table_ref, ahead_ref, out_ref, held_ref):
+def answer_kernel(index_ref, asked_ref, table_ref, ahead_ref, core_ref, out_ref, held_ref):
     width = table_ref.shape[1]
 
     def fetch(r, carry):
@@ -113,17 +107,59 @@
         out_ref[r] = jnp.concatenate([total[:16], total[16:32], total[32:], gap], axis=1)
 
 
-def answers(asked, table, ahead):
+def answers(asked, table, ahead, core):
     width = table.shape[1]
     return pl.pallas_call(
         answer_kernel,
-        in_specs=[SMEM, VMEM, VMEM, pl.BlockSpec(memory_space=pl.ANY)],
+        in_specs=[SMEM, VMEM, VMEM, ANY, ANY],
         out_specs=VMEM,
         out_shape=jax.ShapeDtypeStruct((N_ROW, 16, 128), jnp.float32),
         scratch_shapes=[pltpu.VMEM((N_ROW, ROOM, width), jnp.float32)],
         compiler_params=SMALL,
         name="answers",
-    )(asked, asked, table, ahead)
+    )(asked, asked, table, ahead, core)
+
+
+def split(value):
+    lead = value.astype(jnp.bfloat16)
+    return lead, (value - lead.astype(jnp.float32)).astype(jnp.bfloat16)
+
+
+def gradient_kernel(pre_ref, grad_ref, own_ref, part_ref, hidden_ref, out_ref):
+    width, hid = own_ref.shape[0], pre_ref.shape[1]
+    turned = part_ref[...].T
+    agg = jnp.concatenate([turned[k * width : (k + 1) * width] for k in range(DST // 16)], axis=1)
+    lead, rest = split(jnp.concatenate([own_ref[...], agg], axis=0))
+    both = jnp.concatenate([lead, rest], axis=0)
+    step = 256
+    for at in range(hid // step):
+        value = pre_ref[:, at * step : (at + 1) * step]
+        square = value * value
+        bent = jnp.tanh(BEND * (value + CUBE * (value * square)))
+        hidden_ref[:, at * step : (at + 1) * step] = (0.5 * value) * (1.0 + bent)
+        slope = 0.5 * (1.0 + bent) + (0.5 * value) * (1.0 - bent * bent) * (BEND * (1.0 + (3.0 * CUBE) * square))
+        high, low = split(grad_ref[:, at * step : (at + 1) * step] * slope)
+        total = jnp.dot(both, high, preferred_element_type=jnp.float32)
+        total = total[: 2 * width] + total[2 * width :] + jnp.dot(lead, low, preferred_element_type=jnp.float32)
+        for line in range(4):
+            for lane in range(step // 128):
+                out_ref[line * (hid // 128) + at * (step // 128) + lane] = total[
+                    line * 16 : line * 16 + 16, lane * 128 : lane * 128 + 128
+                ]
+
+
+def gradients(pre, grad_out, own, part):
+    return pl.pallas_call(
+        gradient_kernel,
+        in_specs=[VMEM] * 4,
+        out_specs=[VMEM] * 2,
+        out_shape=[
+            jax.ShapeDtypeStruct(pre.shape, jnp.float32),
+            jax.ShapeDtypeStruct((N_ROW, 16, 128), jnp.float32),
+        ],
+        compiler_params=SMALL,
+        name="gradients",
+    )(pre, grad_out, own, part)
 
 
 def body(features, dest_feat, owner, local_row, w_self, w_neigh, grad_out):
@@ -132,22 +168,19 @@
     asked = requests(owner.reshape(1, -1), local_row.reshape(1, -1))
     asked = exchange(asked.reshape(N_ROW, 2, SLOTS), ROW).reshape(2 * N_ROW, SLOTS)
     pre_self = jnp.dot(dest_feat, w_self, precision=HIGH)
-    part = exchange(answers(asked, features, pre_self), ROW)
+    core = lax.axis_index("core")
+    part = exchange(answers(asked, features, pre_self, core.reshape(1)), ROW)
     part = jnp.sum(part, axis=0) / FAN
     agg = jnp.concatenate([part[:, k * width : (k + 1) * width] for k in range(DST // 16)], axis=0)
     pre = pre_self + jnp.dot(agg, w_neigh, precision=HIGH)
     pair = lax.all_gather(pre.reshape(2, DST // 2, hid), "core", axis=0, tiled=False)
-    half = jnp.sum(lax.dynamic_index_in_dim(pair, lax.axis_index("core"), axis=1, keepdims=False), axis=0)
+    half = jnp.sum(lax.dynamic_index_in_dim(pair, core, axis=1, keepdims=False, allow_negative_indices=False), axis=0)
     half = half.reshape(3, 8, 4, 256).transpose(0, 2, 1, 3).reshape(N_Z, 8, 256)
     tile = jnp.sum(exchange(half, "z"), axis=0)
     half = exchange(jnp.broadcast_to(tile[None], (N_Z, 8, 256)), "z")
     half = half.reshape(3, 4, 8, 256).transpose(0, 2, 1, 3).reshape(DST // 2, hid)
     pre = lax.all_gather(half, "core", axis=0, tiled=True)
-    hidden, slope = activate(pre)
-    dpre = grad_out * slope
-    both = jnp.concatenate([dest_feat.T, agg.T], axis=0)
-    part = jnp.dot(both, dpre, precision=HIGH)
-    part = part.reshape(4, 16, 8, 128).transpose(0, 2, 1, 3).reshape(N_ROW, 16, 128)
+    hidden, part = gradients(pre, grad_out, dest_feat.T, part)
     total = jnp.sum(exchange(part, ROW), axis=0)
     grads = exchange(jnp.broadcast_to(total[None], (N_ROW, 16, 128)), ROW)
     grads = grads.reshape(4, 8, 16, 128).transpose(0, 2, 1, 3).reshape(64, hid)

time: 126 us -> 122 us (0.968)
  blocking collectives: 44.9 us -> 90.1 us
  waiting for transfers between devices: 39.1 us -> 6.08 us
  starting transfers between devices: 26.1 us -> 13 us
  local copies, waits for them, and re-layouts: 5.55 us -> 4.05 us
    all_to_all x2 -> x5, blocking collectives: 40.9 us -> 86.1 us  [exchange(): return lax.all_to_all(value, axis, split_axis=0, concat_axis=0, tiled=True)]
    all_to_all x4 -> x1, waiting for transfers between devices: 39.1 us -> 6.08 us  [exchange(): return lax.all_to_all(value, axis, split_axis=0, concat_axis=0, tiled=True)]
    all_to_all x4 -> x1, starting transfers between devices: 26.1 us -> 13 us  [exchange(): return lax.all_to_all(value, axis, split_axis=0, concat_axis=0, tiled=True)]
    pallas_call x1 -> x2, Pallas kernels: 4.81 us -> 4.99 us  [the longest x1 4.12 us: answers(): pl.pallas_call(answer_kernel, in_specs=[SMEM, VMEM, VMEM, ANY, ANY], out_...]
  transfers between devices with their start and end apart: 4 -> 1, of which waited for: 4 -> 1; matrix products, arithmetic and copies ran while one was open for 3% -> 2% of each run, Pallas kernels for 0% -> 0%
where the time goes in v5:
time: 122 us
  blocking collectives  90.1 us (74%)
  starting transfers between devices  13 us (11%)
  Pallas kernels  6.26 us (5%)
  waiting for transfers between devices  6.08 us (5%)
  local copies, waits for them, and re-layouts  4.05 us (3%)
    all_to_all x5, blocking collectives, exchange(): return lax.all_to_all(value, axis, split_axis=0, concat_axis=0, tiled=True)  86.1 us
    all_to_all x1, starting transfers between devices, exchange(): return lax.all_to_all(value, axis, split_axis=0, concat_axis=0, tiled=True)  13 us
    all_to_all x1, waiting for transfers between devices, exchange(): return lax.all_to_all(value, axis, split_axis=0, concat_axis=0, tiled=True)  6.08 us
    pallas_call x1, Pallas kernels, answers(): pl.pallas_call(answer_kernel, in_specs=[SMEM, VMEM, VMEM, ANY, ANY], out_...  4.12 us
  transfers between devices with their start and end apart: 1, of which 1 were waited for; matrix products, arithmetic and copies ran while one was open for 2% of the time, Pallas kernels for 0%

profile of v5, /device:TPU:8, one launch (start us, length us, event | category | flops | bytes accessed | tf_op | source)
XLA Modules:
  0.0 121.6 jit_solution(7133730421977857897)
XLA Ops:
  0.6 0.0 copy-start
  0.6 0.7 reshape.42.row_ref
  1.4 0.0 copy-start.3
  1.4 0.7 copy-done.3
  2.1 1.3 %requests.1 = s32[64,128]{1,0:T(8,128)} custom-call(s32[1,1200]{1,0:T(1,128)S(1)} %bitcast.33, s32[1,1200]{1,0:T(1,128)S(1)} %reshape.42.row_ref), custom_call_target="tpu_custom_call" | custom-call | tf_op jit(solution)/shard_map/requests/pallas_call | solution.py:77
  3.3 13.0 %all-to-all-start = ((s32[32,2,128]{2,1,0:T(2,128)}), s32[32,2,128]{2,1,0:T(2,128)S(1)}, u32[]{:S(2)}, u32[]{:S(2)}) async-start(s32[32,2,128]{2,1,0:T(2,128)} %bitcast.1), calls=%async_computation | async-start | bytes 65536 | tf_op jit(solution)/shard_map/all_to_all | solution.py:28
  16.3 0.0 copy-done
  16.3 1.0 fusion.8.ahead_ref
  17.4 1.6 %copy.18.table_ref = f32[4096,32]{1,0:T(8,128)S(1)} copy(f32[4096,32]{0,1:T(8,128)} %param.7) | data formatting | bytes 1048576 | tf_op args[0]
  19.0 0.0 copy-start.4
  19.0 6.1 %all-to-all-done = s32[32,2,128]{2,1,0:T(2,128)S(1)} async-done(((s32[32,2,128]{2,1,0:T(2,128)}), s32[32,2,128]{2,1,0:T(2,128)S(1)}, u32[]{:S(2)}, u32[]{:S(2)}) %all-to-all-start) | async-done | bytes 32800 | tf_op jit(solution)/shard_map/all_to_all | solution.py:28
  25.1 4.1 %answers.1 = f32[32,16,128]{2,1,0:T(8,128)S(1)} custom-call(s32[64,128]{1,0:T(8,128)S(1)} %bitcast.30, s32[64,128]{1,0:T(8,128)S(1)} %bitcast.31, f32[4096,32]{1,0:T(8,128)S(1)} %copy.18.table_ref, f32[48,1024]{1,0:T(8,128)S(1)} %fusion.8.ahead_ref, s32[1]{0:T(128)} %bitcast.3.core_ref), custom_call_target="tpu_custom_call" | custom-call | tf_op jit(solution)/shard_map/answers/pallas_call | solution.py:112
  29.2 0.0 copy-start.1
  29.2 0.0 copy-start.2
  29.2 15.0 %all_to_all.30 = f32[32,16,128]{2,1,0:T(8,128)S(1)} all-to-all(f32[32,16,128]{2,1,0:T(8,128)S(1)} %answers.1), channel_id=1, replica_groups=mesh['y'=8,'x'=4,'z'=12,'core'=2] {'y','x'}, dimensions={0} | all-to-all | bytes 524288 | tf_op jit(solution)/shard_map/all_to_all | solution.py:28
  44.3 0.1 fusion.7
  44.4 0.0 copy-done.4
  44.4 0.2 convolution_add_fusion
  44.6 2.1 %all_gather.6 = f32[2,2,24,1024]{3,2,1,0:T(8,128)S(1)} all-gather(f32[1,2,24,1024]{3,2,1,0:T(8,128)S(1)} %bitcast.35), channel_id=1, replica_groups=mesh['y'=8,'x'=4,'z'=12,'core'=2] {'core'}, dimensions={0}, use_global_device_ids=true | all-gather | bytes 589824 | tf_op jit(solution)/shard_map/all_gather | solution.py:176
  46.7 23.9 %all_to_all.31 = f32[12,8,256]{2,1,0:T(8,128)S(1)} all-to-all(f32[12,8,256]{2,1,0:T(8,128)S(1)} %bitcast.38), channel_id=1, replica_groups=mesh['y'=8,'x'=4,'z'=12,'core'=2] {'z'}, dimensions={0} | all-to-all | bytes 196608 | tf_op jit(solution)/shard_map/all_to_all | solution.py:28
  70.7 14.3 %all_to_all.32 = f32[12,8,256]{2,1,0:T(8,128)S(1)} all-to-all(f32[12,8,256]{2,1,0:T(8,128)S(1)} %broadcast_in_dim.4), channel_id=1, replica_groups=mesh['y'=8,'x'=4,'z'=12,'core'=2] {'z'}, dimensions={0} | all-to-all | bytes 196608 | tf_op jit(solution)/shard_map/all_to_all | solution.py:28
  85.0 1.9 %all_gather.7.pre_ref = f32[48,1024]{1,0:T(8,128)S(1)} all-gather(f32[24,1024]{1,0:T(8,128)S(1)} %bitcast.39), channel_id=1, replica_groups=mesh['y'=8,'x'=4,'z'=12,'core'=2] {'core'}, dimensions={0}, use_global_device_ids=true | all-gather | bytes 294912 | tf_op jit(solution)/shard_map/all_gather | solution.py:182
  86.9 0.0 copy-done.1
  86.9 0.0 copy-done.2
  86.9 0.9 gradients.1
  87.8 16.9 %all_to_all.33 = f32[32,16,128]{2,1,0:T(8,128)S(1)} all-to-all(f32[32,16,128]{2,1,0:T(8,128)S(1)} %get-tuple-element.6), channel_id=1, replica_groups=mesh['y'=8,'x'=4,'z'=12,'core'=2] {'y','x'}, dimensions={0} | all-to-all | bytes 524288 | tf_op jit(solution)/shard_map/all_to_all | solution.py:28
  104.8 15.9 %all_to_all.34 = f32[32,16,128]{2,1,0:T(8,128)S(1)} all-to-all(f32[32,16,128]{2,1,0:T(8,128)S(1)} %broadcast_in_dim.5), channel_id=1, replica_groups=mesh['y'=8,'x'=4,'z'=12,'core'=2] {'y','x'}, dimensions={0} | all-to-all | bytes 524288 | tf_op jit(solution)/shard_map/all_to_all | solution.py:28
  120.8 0.7 copy_bitcast_fusion
  (10 shorter events, 0.2 us)
Async XLA Ops:
  0.6 15.7 %copy-start = (f32[32,1024]{1,0:T(8,128)S(1)}, f32[32,1024]{1,0:T(8,128)}, u32[]{:S(2)}) copy-start(f32[32,1024]{1,0:T(8,128)} %param.11) | copy-start | bytes 393220
  1.4 0.7 copy-start.3
  3.3 21.8 %all-to-all-start = ((s32[32,2,128]{2,1,0:T(2,128)}), s32[32,2,128]{2,1,0:T(2,128)S(1)}, u32[]{:S(2)}, u32[]{:S(2)}) async-start(s32[32,2,128]{2,1,0:T(2,128)} %bitcast.1), calls=%async_computation | async-start | bytes 65536 | tf_op jit(solution)/shard_map/all_to_all | solution.py:28
  19.0 25.4 %copy-start.4 = (f32[32,1024]{1,0:T(8,128)S(1)}, f32[32,1024]{1,0:T(8,128)}, u32[]{:S(2)}) copy-start(f32[32,1024]{1,0:T(8,128)} %param.12) | copy-start | bytes 393220
  29.2 57.7 %copy-start.1 = (f32[48,1024]{1,0:T(8,128)S(1)}, f32[48,1024]{1,0:T(8,128)}, u32[]{:S(2)}) copy-start(f32[48,1024]{1,0:T(8,128)} %grad_ref.1) | copy-start | bytes 589828
  29.2 57.7 %copy-start.2 = (f32[48,32]{0,1:T(8,128)S(1)}, f32[48,32]{0,1:T(8,128)}, u32[]{:S(2)}) copy-start(f32[48,32]{0,1:T(8,128)} %param.8) | copy-start | bytes 18436

commit v6 on v5

--- a/solution.py
+++ b/solution.py
@@ -16,10 +16,10 @@
 N_Z = 12
 BEND = 0.7978845608
 CUBE = 0.044715
-HIGH = lax.Precision.HIGH
 LANES = (((1,), (1,)), ((), ()))
 VMEM = pl.BlockSpec(memory_space=pltpu.VMEM)
 ANY = pl.BlockSpec(memory_space=pl.ANY)
+HBM = pl.BlockSpec(memory_space=pltpu.HBM)
 SMEM = pl.BlockSpec(memory_space=pltpu.SMEM)
 SMALL = pltpu.CompilerParams(vmem_limit_bytes=16 << 20)
 
@@ -28,7 +28,13 @@
     return lax.all_to_all(value, axis, split_axis=0, concat_axis=0, tiled=True)
 
 
-def request_kernel(owner_ref, row_ref, out_ref):
+def request_kernel(owner_from, row_from, out_ref, owner_ref, row_ref, sems):
+    loads = [
+        pltpu.make_async_copy(owner_from, owner_ref, sems.at[0]),
+        pltpu.make_async_copy(row_from, row_ref, sems.at[1]),
+    ]
+    for load in loads:
+        load.start()
     samples = owner_ref.shape[1]
     blocks = -(-samples // 128)
     line = lax.broadcasted_iota(jnp.int32, (2 * N_ROW, 128), 0)
@@ -38,16 +44,18 @@
     before = jnp.where(before, 1.0, 0.0).astype(jnp.bfloat16)
     slot = lax.broadcasted_iota(jnp.int32, (SLOTS, 128), 0).astype(jnp.float32)
 
-    def part(ref, block, fill):
-        width = min(128, samples - block * 128)
-        values = ref[:, block * 128 : block * 128 + width]
+    def padded(values, fill):
+        width = values.shape[1]
         if width < 128:
             values = jnp.concatenate([values, jnp.full((1, 128 - width), fill, jnp.int32)], axis=1)
         return values
 
+    for load in loads:
+        load.wait()
     marks, counts = [], []
     for block in range(blocks):
-        mark = part(owner_ref, block, -1) == (line >> 1)
+        end = min(samples, block * 128 + 128)
+        mark = padded(owner_ref[:, block * 128 : end], -1) == (line >> 1)
         marks.append(mark)
         counts.append(
             lax.dot_general(
@@ -57,7 +65,8 @@
     seen = jnp.full((2 * N_ROW, 1), -1.0, jnp.float32)
     lefts, rights = [], []
     for block in range(blocks):
-        rows = part(row_ref, block, 0)
+        end = min(samples, block * 128 + 128)
+        rows = padded(row_ref[block * 128 : end].reshape(1, -1), 0)
         mark, count = marks[block], counts[block]
         rank = jnp.sum(jnp.where(mark & even, count + seen, 0.0), axis=0, keepdims=True)
         seen = seen + count[:, 127:128]
@@ -76,15 +85,19 @@
 def requests(owner, local_row):
     return pl.pallas_call(
         request_kernel,
-        in_specs=[VMEM, VMEM],
+        in_specs=[HBM, HBM],
         out_specs=VMEM,
         out_shape=jax.ShapeDtypeStruct((2 * N_ROW, SLOTS), jnp.int32),
-        compiler_params=SMALL,
+        scratch_shapes=[
+            pltpu.VMEM(owner.shape, jnp.int32),
+            pltpu.VMEM(local_row.shape, jnp.int32),
+            pltpu.SemaphoreType.DMA((2,)),
+        ],
         name="requests",
     )(owner, local_row)
 
 
-def answer_kernel(index_ref, asked_ref, table_ref, ahead_ref, core_ref, out_ref, held_ref):
+def answer_kernel(index_ref, asked_ref, table_ref, core_ref, out_ref, held_ref):
     width = table_ref.shape[1]
 
     def fetch(r, carry):
@@ -107,22 +120,59 @@
         out_ref[r] = jnp.concatenate([total[:16], total[16:32], total[32:], gap], axis=1)
 
 
-def answers(asked, table, ahead, core):
+def answers(asked, table, core):
     width = table.shape[1]
     return pl.pallas_call(
         answer_kernel,
-        in_specs=[SMEM, VMEM, VMEM, ANY, ANY],
+        in_specs=[SMEM, VMEM, VMEM, ANY],
         out_specs=VMEM,
         out_shape=jax.ShapeDtypeStruct((N_ROW, 16, 128), jnp.float32),
         scratch_shapes=[pltpu.VMEM((N_ROW, ROOM, width), jnp.float32)],
         compiler_params=SMALL,
         name="answers",
-    )(asked, asked, table, ahead, core)
+    )(asked, asked, table, core)
 
 
 def split(value):
     lead = value.astype(jnp.bfloat16)
     return lead, (value - lead.astype(jnp.float32)).astype(jnp.bfloat16)
+
+
+def product(left, right):
+    lead, rest = split(left)
+    high, low = split(right)
+    total = jnp.dot(jnp.concatenate([lead, rest], axis=0), high, preferred_element_type=jnp.float32)
+    lines = left.shape[0]
+    return total[:lines] + total[lines:] + jnp.dot(lead, low, preferred_element_type=jnp.float32)
+
+
+def project_kernel(part_ref, own_ref, self_ref, neigh_ref, agg_ref, out_ref):
+    width, hid = self_ref.shape
+    total = part_ref[0]
+    for r in range(1, N_ROW):
+        total = total + part_ref[r]
+    total = total / FAN
+    agg_ref[...] = total
+    agg = jnp.concatenate([total[:, k * width : (k + 1) * width] for k in range(DST // 16)], axis=0)
+    both = jnp.concatenate([own_ref[...].T, agg], axis=1)
+    step = 256
+    for at in range(0, hid, step):
+        weight = jnp.concatenate([self_ref[:, at : at + step], neigh_ref[:, at : at + step]], axis=0)
+        out_ref[:, at : at + step] = product(both, weight)
+
+
+def project(part, own, w_self, w_neigh):
+    return pl.pallas_call(
+        project_kernel,
+        in_specs=[VMEM] * 4,
+        out_specs=[VMEM] * 2,
+        out_shape=[
+            jax.ShapeDtypeStruct(part.shape[1:], jnp.float32),
+            jax.ShapeDtypeStruct((DST, w_self.shape[1]), jnp.float32),
+        ],
+        compiler_params=SMALL,
+        name="project",
+    )(part, own, w_self, w_neigh)
 
 
 def gradient_kernel(pre_ref, grad_ref, own_ref, part_ref, hidden_ref, out_ref):
@@ -163,16 +213,13 @@
 
 
 def body(features, dest_feat, owner, local_row, w_self, w_neigh, grad_out):
-    width = features.shape[1]
     hid = w_self.shape[1]
-    asked = requests(owner.reshape(1, -1), local_row.reshape(1, -1))
+    asked = requests(owner.reshape(1, -1), local_row)
     asked = exchange(asked.reshape(N_ROW, 2, SLOTS), ROW).reshape(2 * N_ROW, SLOTS)
-    pre_self = jnp.dot(dest_feat, w_self, precision=HIGH)
     core = lax.axis_index("core")
-    part = exchange(answers(asked, features, pre_self, core.reshape(1)), ROW)
-    part = jnp.sum(part, axis=0) / FAN
-    agg = jnp.concatenate([part[:, k * width : (k + 1) * width] for k in range(DST // 16)], axis=0)
-    pre = pre_self + jnp.dot(agg, w_neigh, precision=HIGH)
+    own = dest_feat.T
+    part = exchange(answers(asked, features, core.reshape(1)), ROW)
+    agg, pre = project(part, own, w_self, w_neigh)
     pair = lax.all_gather(pre.reshape(2, DST // 2, hid), "core", axis=0, tiled=False)
     half = jnp.sum(lax.dynamic_index_in_dim(pair, core, axis=1, keepdims=False, allow_negative_indices=False), axis=0)
     half = half.reshape(3, 8, 4, 256).transpose(0, 2, 1, 3).reshape(N_Z, 8, 256)
@@ -180,7 +227,7 @@
     half = exchange(jnp.broadcast_to(tile[None], (N_Z, 8, 256)), "z")
     half = half.reshape(3, 4, 8, 256).transpose(0, 2, 1, 3).reshape(DST // 2, hid)
     pre = lax.all_gather(half, "core", axis=0, tiled=True)
-    hidden, part = gradients(pre, grad_out, dest_feat.T, part)
+    hidden, part = gradients(pre, grad_out, own, agg)
     total = jnp.sum(exchange(part, ROW), axis=0)
     grads = exchange(jnp.broadcast_to(total[None], (N_ROW, 16, 128)), ROW)
     grads = grads.reshape(4, 8, 16, 128).transpose(0, 2, 1, 3).reshape(64, hid)

time: 122 us -> 121 us (level)
  local copies, waits for them, and re-layouts: 4.05 us -> 2.54 us
    pallas_call x2 -> x3, Pallas kernels: 5.39 us -> 6.48 us  [the longest x1 4.12 us: answers(): pl.pallas_call(answer_kernel, in_specs=[SMEM, VMEM, VMEM, ANY], out_specs...]
  transfers between devices with their start and end apart: 1 -> 1, of which waited for: 1 -> 1; matrix products, arithmetic and copies ran while one was open for 2% -> 1% of each run, Pallas kernels for 0% -> 0%
where the time goes in v6:
time: 121 us
  blocking collectives  90 us (74%)
  starting transfers between devices  13 us (11%)
  Pallas kernels  7.35 us (6%)
  waiting for transfers between devices  7.07 us (6%)
  local copies, waits for them, and re-layouts  2.54 us (2%)
    all_to_all x5, blocking collectives, exchange(): return lax.all_to_all(value, axis, split_axis=0, concat_axis=0, tiled=True)  85.9 us
    all_to_all x1, starting transfers between devices, exchange(): return lax.all_to_all(value, axis, split_axis=0, concat_axis=0, tiled=True)  13 us
    all_to_all x1, waiting for transfers between devices, exchange(): return lax.all_to_all(value, axis, split_axis=0, concat_axis=0, tiled=True)  7.07 us
    pallas_call x1, Pallas kernels, answers(): pl.pallas_call(answer_kernel, in_specs=[SMEM, VMEM, VMEM, ANY], out_specs...  4.12 us
  transfers between devices with their start and end apart: 1, of which 1 were waited for; matrix products, arithmetic and copies ran while one was open for 1% of the time, Pallas kernels for 0%

profile of v6, /device:TPU:8, one launch (start us, length us, event | category | flops | bytes accessed | tf_op | source)
XLA Modules:
  0.0 120.7 jit_solution(14712541723590709441)
XLA Ops:
  0.6 2.0 %requests.1 = s32[64,128]{1,0:T(8,128)} custom-call(s32[1,1200]{1,0:T(1,128)} %bitcast.38, s32[1200]{0:T(1024)} %row_from.1), custom_call_target="tpu_custom_call" | custom-call | tf_op jit(solution)/shard_map/requests/pallas_call | solution.py:86
  2.6 13.0 %all-to-all-start = ((s32[32,2,128]{2,1,0:T(2,128)}), s32[32,2,128]{2,1,0:T(2,128)S(1)}, u32[]{:S(2)}, u32[]{:S(2)}) async-start(s32[32,2,128]{2,1,0:T(2,128)} %bitcast.37), calls=%async_computation | async-start | bytes 65536 | tf_op jit(solution)/shard_map/all_to_all | solution.py:28
  15.6 1.6 %copy.18.table_ref = f32[4096,32]{1,0:T(8,128)S(1)} copy(f32[4096,32]{0,1:T(8,128)} %param.7) | data formatting | bytes 1048576 | tf_op args[0]
  17.3 0.0 copy-start.1
  17.3 0.0 copy-start.2
  17.3 0.0 copy-start.3
  17.3 7.1 %all-to-all-done = s32[32,2,128]{2,1,0:T(2,128)S(1)} async-done(((s32[32,2,128]{2,1,0:T(2,128)}), s32[32,2,128]{2,1,0:T(2,128)S(1)}, u32[]{:S(2)}, u32[]{:S(2)}) %all-to-all-start) | async-done | bytes 32800 | tf_op jit(solution)/shard_map/all_to_all | solution.py:28
  24.4 0.0 copy-start
  24.4 4.1 %answers.1 = f32[32,16,128]{2,1,0:T(8,128)S(1)} custom-call(s32[64,128]{1,0:T(8,128)S(1)} %bitcast.27, s32[64,128]{1,0:T(8,128)S(1)} %bitcast.28, f32[4096,32]{1,0:T(8,128)S(1)} %copy.18.table_ref, s32[1]{0:T(128)} %bitcast.3.core_ref), custom_call_target="tpu_custom_call" | custom-call | tf_op jit(solution)/shard_map/answers/pallas_call | solution.py:125
  28.5 14.9 %all_to_all.30.part_ref = f32[32,16,128]{2,1,0:T(8,128)S(1)} all-to-all(f32[32,16,128]{2,1,0:T(8,128)S(1)} %answers.1), channel_id=1, replica_groups=mesh['y'=8,'x'=4,'z'=12,'core'=2] {'y','x'}, dimensions={0} | all-to-all | bytes 524288 | tf_op jit(solution)/shard_map/all_to_all | solution.py:28
  43.4 0.0 copy-done.1
  43.4 0.0 copy-done.2
  43.4 0.0 copy-done.3
  43.4 0.4 project.1
  43.8 2.1 %all_gather.6 = f32[2,2,24,1024]{3,2,1,0:T(8,128)S(1)} all-gather(f32[1,2,24,1024]{3,2,1,0:T(8,128)S(1)} %bitcast.29), channel_id=1, replica_groups=mesh['y'=8,'x'=4,'z'=12,'core'=2] {'core'}, dimensions={0}, use_global_device_ids=true | all-gather | bytes 589824 | tf_op jit(solution)/shard_map/all_gather | solution.py:223
  45.9 24.0 %all_to_all.31 = f32[12,8,256]{2,1,0:T(8,128)S(1)} all-to-all(f32[12,8,256]{2,1,0:T(8,128)S(1)} %bitcast.35), channel_id=1, replica_groups=mesh['y'=8,'x'=4,'z'=12,'core'=2] {'z'}, dimensions={0} | all-to-all | bytes 196608 | tf_op jit(solution)/shard_map/all_to_all | solution.py:28
  69.9 14.3 %all_to_all.32 = f32[12,8,256]{2,1,0:T(8,128)S(1)} all-to-all(f32[12,8,256]{2,1,0:T(8,128)S(1)} %broadcast_in_dim.4), channel_id=1, replica_groups=mesh['y'=8,'x'=4,'z'=12,'core'=2] {'z'}, dimensions={0} | all-to-all | bytes 196608 | tf_op jit(solution)/shard_map/all_to_all | solution.py:28
  84.2 1.9 %all_gather.7.pre_ref = f32[48,1024]{1,0:T(8,128)S(1)} all-gather(f32[24,1024]{1,0:T(8,128)S(1)} %bitcast.36), channel_id=1, replica_groups=mesh['y'=8,'x'=4,'z'=12,'core'=2] {'core'}, dimensions={0}, use_global_device_ids=true | all-gather | bytes 294912 | tf_op jit(solution)/shard_map/all_gather | solution.py:229
  86.1 0.0 copy-done
  86.1 0.9 gradients.1
  87.0 16.9 %all_to_all.33 = f32[32,16,128]{2,1,0:T(8,128)S(1)} all-to-all(f32[32,16,128]{2,1,0:T(8,128)S(1)} %get-tuple-element.10), channel_id=1, replica_groups=mesh['y'=8,'x'=4,'z'=12,'core'=2] {'y','x'}, dimensions={0} | all-to-all | bytes 524288 | tf_op jit(solution)/shard_map/all_to_all | solution.py:28
  103.9 15.9 %all_to_all.34 = f32[32,16,128]{2,1,0:T(8,128)S(1)} all-to-all(f32[32,16,128]{2,1,0:T(8,128)S(1)} %broadcast_in_dim.5), channel_id=1, replica_groups=mesh['y'=8,'x'=4,'z'=12,'core'=2] {'y','x'}, dimensions={0} | all-to-all | bytes 524288 | tf_op jit(solution)/shard_map/all_to_all | solution.py:28
  120.0 0.7 copy_bitcast_fusion
  (8 shorter events, 0.2 us)
Async XLA Ops:
  2.6 21.8 %all-to-all-start = ((s32[32,2,128]{2,1,0:T(2,128)}), s32[32,2,128]{2,1,0:T(2,128)S(1)}, u32[]{:S(2)}, u32[]{:S(2)}) async-start(s32[32,2,128]{2,1,0:T(2,128)} %bitcast.37), calls=%async_computation | async-start | bytes 65536 | tf_op jit(solution)/shard_map/all_to_all | solution.py:28
  17.3 26.1 %copy-start.1 = (f32[32,1024]{1,0:T(8,128)S(1)}, f32[32,1024]{1,0:T(8,128)}, u32[]{:S(2)}) copy-start(f32[32,1024]{1,0:T(8,128)} %self_ref.1) | copy-start | bytes 393220
  17.3 26.1 %copy-start.2 = (f32[32,1024]{1,0:T(8,128)S(1)}, f32[32,1024]{1,0:T(8,128)}, u32[]{:S(2)}) copy-start(f32[32,1024]{1,0:T(8,128)} %neigh_ref.1) | copy-start | bytes 393220
  17.3 26.1 %copy-start.3 = (f32[48,32]{0,1:T(8,128)S(1)}, f32[48,32]{0,1:T(8,128)}, u32[]{:S(2)}) copy-start(f32[48,32]{0,1:T(8,128)} %param.8) | copy-start | bytes 18436
  24.4 61.7 %copy-start = (f32[48,1024]{1,0:T(8,128)S(1)}, f32[48,1024]{1,0:T(8,128)}, u32[]{:S(2)}) copy-start(f32[48,1024]{1,0:T(8,128)} %grad_ref.1) | copy-start | bytes 589828

commit v7 on v6

--- a/solution.py
+++ b/solution.py
@@ -20,7 +20,6 @@
 VMEM = pl.BlockSpec(memory_space=pltpu.VMEM)
 ANY = pl.BlockSpec(memory_space=pl.ANY)
 HBM = pl.BlockSpec(memory_space=pltpu.HBM)
-SMEM = pl.BlockSpec(memory_space=pltpu.SMEM)
 SMALL = pltpu.CompilerParams(vmem_limit_bytes=16 << 20)
 
 
@@ -97,40 +96,48 @@
     )(owner, local_row)
 
 
-def answer_kernel(index_ref, asked_ref, table_ref, core_ref, out_ref, held_ref):
+def answer_kernel(index_from, asked_ref, table_ref, core_ref, out_ref, held_ref, place_ref, index_ref, sem):
     width = table_ref.shape[1]
+    load = pltpu.make_async_copy(index_from, index_ref, sem)
+    load.start()
+    line = lax.broadcasted_iota(jnp.int32, (DST, ROOM), 0) + 1
+    for r in range(N_ROW):
+        dest = asked_ref[2 * r + 1 : 2 * r + 2, :ROOM]
+        place_ref[r] = jnp.where(dest == line, 1.0, 0.0).astype(jnp.bfloat16)
+        held_ref[r, ROOM - 8 :, :] = jnp.zeros((8, width), jnp.float32)
+    load.wait()
 
     def fetch(r, carry):
-        held_ref[r, ROOM - 8 :, :] = jnp.zeros((8, width), jnp.float32)
         for s in range(CAP):
-            held_ref[r, s : s + 1, :] = table_ref[pl.ds(index_ref[2 * r, s], 1), :]
+            held_ref[r, s : s + 1, :] = table_ref[pl.ds(index_ref[r * CAP + s], 1), :]
         return carry
 
     lax.fori_loop(0, N_ROW, fetch, 0)
-    line = lax.broadcasted_iota(jnp.int32, (DST, ROOM), 0) + 1
     gap = jnp.zeros((16, 128 - 3 * width), jnp.float32)
     for r in range(N_ROW):
-        dest = asked_ref[2 * r + 1 : 2 * r + 2, :ROOM]
-        place = jnp.where(dest == line, 1.0, 0.0).astype(jnp.bfloat16)
-        value = held_ref[r]
-        lead = value.astype(jnp.bfloat16)
-        rest = (value - lead.astype(jnp.float32)).astype(jnp.bfloat16)
-        total = jnp.dot(place, jnp.concatenate([lead, rest], axis=1), preferred_element_type=jnp.float32)
+        lead, rest = split(held_ref[r])
+        total = jnp.dot(place_ref[r], jnp.concatenate([lead, rest], axis=1), preferred_element_type=jnp.float32)
         total = total[:, :width] + total[:, width:]
         out_ref[r] = jnp.concatenate([total[:16], total[16:32], total[32:], gap], axis=1)
 
 
 def answers(asked, table, core):
     width = table.shape[1]
+    index = asked.reshape(N_ROW, 2, SLOTS)[:, 0, :CAP].reshape(-1)
     return pl.pallas_call(
         answer_kernel,
-        in_specs=[SMEM, VMEM, VMEM, ANY],
+        in_specs=[VMEM, VMEM, VMEM, ANY],
         out_specs=VMEM,
         out_shape=jax.ShapeDtypeStruct((N_ROW, 16, 128), jnp.float32),
-        scratch_shapes=[pltpu.VMEM((N_ROW, ROOM, width), jnp.float32)],
+        scratch_shapes=[
+            pltpu.VMEM((N_ROW, ROOM, width), jnp.float32),
+            pltpu.VMEM((N_ROW, DST, ROOM), jnp.bfloat16),
+            pltpu.SMEM(index.shape, jnp.int32),
+            pltpu.SemaphoreType.DMA,
+        ],
         compiler_params=SMALL,
         name="answers",
-    )(asked, asked, table, core)
+    )(index, asked, table, core)
 
 
 def split(value):
@@ -212,6 +219,27 @@
     )(pre, grad_out, own, part)
 
 
+def spread_kernel(block_ref, self_ref, neigh_ref):
+    lanes = self_ref.shape[1] // 128
+    for at, out_ref in ((0, self_ref), (1, neigh_ref)):
+        for line in range(2):
+            for lane in range(lanes):
+                out_ref[line * 16 : line * 16 + 16, lane * 128 : lane * 128 + 128] = block_ref[
+                    (2 * at + line) * lanes + lane
+                ]
+
+
+def spread(blocks, hid):
+    return pl.pallas_call(
+        spread_kernel,
+        in_specs=[VMEM],
+        out_specs=[VMEM] * 2,
+        out_shape=[jax.ShapeDtypeStruct((32, hid), jnp.float32)] * 2,
+        compiler_params=SMALL,
+        name="spread",
+    )(blocks)
+
+
 def body(features, dest_feat, owner, local_row, w_self, w_neigh, grad_out):
     hid = w_self.shape[1]
     asked = requests(owner.reshape(1, -1), local_row)
@@ -230,8 +258,7 @@
     hidden, part = gradients(pre, grad_out, own, agg)
     total = jnp.sum(exchange(part, ROW), axis=0)
     grads = exchange(jnp.broadcast_to(total[None], (N_ROW, 16, 128)), ROW)
-    grads = grads.reshape(4, 8, 16, 128).transpose(0, 2, 1, 3).reshape(64, hid)
-    return (hidden, grads[:32], grads[32:])
+    return (hidden, *spread(grads, hid))
 
 
 def solution(mesh):

time: 121 us -> 121 us (level)
    pallas_call x1 -> x2, Pallas kernels: 4.12 us -> 4.46 us  [the longest x1 3.75 us: answers(): pl.pallas_call(answer_kernel, in_specs=[VMEM, VMEM, VMEM, ANY], out_specs...]
where the time goes in v7:
time: 121 us; the launch traced here: 120 us
  blocking collectives  89.9 us (74%)
  starting transfers between devices  13 us (11%)
  Pallas kernels  7.7 us (6%)
  waiting for transfers between devices  7.07 us (6%)
  local copies, waits for them, and re-layouts  1.83 us (2%)
    all_to_all x5, blocking collectives, exchange(): return lax.all_to_all(value, axis, split_axis=0, concat_axis=0, tiled=True)  85.9 us
    all_to_all x1, starting transfers between devices, exchange(): return lax.all_to_all(value, axis, split_axis=0, concat_axis=0, tiled=True)  13 us
    all_to_all x1, waiting for transfers between devices, exchange(): return lax.all_to_all(value, axis, split_axis=0, concat_axis=0, tiled=True)  7.07 us
    pallas_call x1, Pallas kernels, answers(): pl.pallas_call(answer_kernel, in_specs=[VMEM, VMEM, VMEM, ANY], out_specs...  3.75 us
  transfers between devices with their start and end apart: 1, of which 1 were waited for; matrix products, arithmetic and copies ran while one was open for 1% of the time, Pallas kernels for 0%

profile of v7, /device:TPU:8, one launch (start us, length us, event | category | flops | bytes accessed | tf_op | source)
XLA Modules:
  0.0 120.4 jit_solution(12204469732073802076)
XLA Ops:
  0.6 2.0 %requests.1 = s32[64,128]{1,0:T(8,128)} custom-call(s32[1,1200]{1,0:T(1,128)} %bitcast.23, s32[1200]{0:T(1024)} %row_from.1), custom_call_target="tpu_custom_call" | custom-call | tf_op jit(solution)/shard_map/requests/pallas_call | solution.py:85
  2.6 13.0 %all-to-all-start = ((s32[32,2,128]{2,1,0:T(2,128)}), s32[32,2,128]{2,1,0:T(2,128)S(1)}, u32[]{:S(2)}, u32[]{:S(2)}) async-start(s32[32,2,128]{2,1,0:T(2,128)} %bitcast.22), calls=%async_computation | async-start | bytes 65536 | tf_op jit(solution)/shard_map/all_to_all | solution.py:27
  15.6 1.6 %copy.12.table_ref = f32[4096,32]{1,0:T(8,128)S(1)} copy(f32[4096,32]{0,1:T(8,128)} %param.7) | data formatting | bytes 1048576 | tf_op args[0]
  17.3 0.0 copy-start.1
  17.3 0.0 copy-start.2
  17.3 0.0 copy-start.3
  17.3 7.1 %all-to-all-done = s32[32,2,128]{2,1,0:T(2,128)S(1)} async-done(((s32[32,2,128]{2,1,0:T(2,128)}), s32[32,2,128]{2,1,0:T(2,128)S(1)}, u32[]{:S(2)}, u32[]{:S(2)}) %all-to-all-start) | async-done | bytes 32800 | tf_op jit(solution)/shard_map/all_to_all | solution.py:27
  24.4 0.1 reshape_squeeze.3.index_from
  24.5 0.0 copy-start
  24.6 3.7 %answers.1 = f32[32,16,128]{2,1,0:T(8,128)S(1)} custom-call(s32[2400]{0:T(1024)S(1)} %reshape_squeeze.3.index_from, s32[64,128]{1,0:T(8,128)S(1)} %bitcast.16, f32[4096,32]{1,0:T(8,128)S(1)} %copy.12.table_ref, s32[1]{0:T(128)} %bitcast.3.core_ref), custom_call_target="tpu_custom_call" | custom-call | tf_op jit(solution)/shard_map/answers/pallas_call | solution.py:127
  28.3 14.9 %all_to_all.30.part_ref = f32[32,16,128]{2,1,0:T(8,128)S(1)} all-to-all(f32[32,16,128]{2,1,0:T(8,128)S(1)} %answers.1), channel_id=1, replica_groups=mesh['y'=8,'x'=4,'z'=12,'core'=2] {'y','x'}, dimensions={0} | all-to-all | bytes 524288 | tf_op jit(solution)/shard_map/all_to_all | solution.py:27
  43.2 0.0 copy-done.1
  43.2 0.0 copy-done.2
  43.2 0.0 copy-done.3
  43.2 0.4 project.1
  43.6 2.1 %all_gather.6 = f32[2,2,24,1024]{3,2,1,0:T(8,128)S(1)} all-gather(f32[1,2,24,1024]{3,2,1,0:T(8,128)S(1)} %bitcast.17), channel_id=1, replica_groups=mesh['y'=8,'x'=4,'z'=12,'core'=2] {'core'}, dimensions={0}, use_global_device_ids=true | all-gather | bytes 589824 | tf_op jit(solution)/shard_map/all_gather | solution.py:251
  45.7 24.0 %all_to_all.31 = f32[12,8,256]{2,1,0:T(8,128)S(1)} all-to-all(f32[12,8,256]{2,1,0:T(8,128)S(1)} %bitcast.20), channel_id=1, replica_groups=mesh['y'=8,'x'=4,'z'=12,'core'=2] {'z'}, dimensions={0} | all-to-all | bytes 196608 | tf_op jit(solution)/shard_map/all_to_all | solution.py:27
  69.7 14.3 %all_to_all.32 = f32[12,8,256]{2,1,0:T(8,128)S(1)} all-to-all(f32[12,8,256]{2,1,0:T(8,128)S(1)} %broadcast_in_dim.4), channel_id=1, replica_groups=mesh['y'=8,'x'=4,'z'=12,'core'=2] {'z'}, dimensions={0} | all-to-all | bytes 196608 | tf_op jit(solution)/shard_map/all_to_all | solution.py:27
  83.9 1.9 %all_gather.7.pre_ref = f32[48,1024]{1,0:T(8,128)S(1)} all-gather(f32[24,1024]{1,0:T(8,128)S(1)} %bitcast.21), channel_id=1, replica_groups=mesh['y'=8,'x'=4,'z'=12,'core'=2] {'core'}, dimensions={0}, use_global_device_ids=true | all-gather | bytes 294912 | tf_op jit(solution)/shard_map/all_gather | solution.py:257
  85.9 0.0 copy-done
  85.9 0.9 gradients.1
  86.8 16.9 %all_to_all.33 = f32[32,16,128]{2,1,0:T(8,128)S(1)} all-to-all(f32[32,16,128]{2,1,0:T(8,128)S(1)} %get-tuple-element.12), channel_id=1, replica_groups=mesh['y'=8,'x'=4,'z'=12,'core'=2] {'y','x'}, dimensions={0} | all-to-all | bytes 524288 | tf_op jit(solution)/shard_map/all_to_all | solution.py:27
  103.7 15.9 %all_to_all.34.block_ref = f32[32,16,128]{2,1,0:T(8,128)S(1)} all-to-all(f32[32,16,128]{2,1,0:T(8,128)S(1)} %broadcast_in_dim.5), channel_id=1, replica_groups=mesh['y'=8,'x'=4,'z'=12,'core'=2] {'y','x'}, dimensions={0} | all-to-all | bytes 524288 | tf_op jit(solution)/shard_map/all_to_all | solution.py:27
  119.6 0.7 spread.1
  (6 shorter events, 0.1 us)
Async XLA Ops:
  2.6 21.8 %all-to-all-start = ((s32[32,2,128]{2,1,0:T(2,128)}), s32[32,2,128]{2,1,0:T(2,128)S(1)}, u32[]{:S(2)}, u32[]{:S(2)}) async-start(s32[32,2,128]{2,1,0:T(2,128)} %bitcast.22), calls=%async_computation | async-start | bytes 65536 | tf_op jit(solution)/shard_map/all_to_all | solution.py:27
  17.3 25.9 %copy-start.1 = (f32[32,1024]{1,0:T(8,128)S(1)}, f32[32,1024]{1,0:T(8,128)}, u32[]{:S(2)}) copy-start(f32[32,1024]{1,0:T(8,128)} %self_ref.1) | copy-start | bytes 393220
  17.3 25.9 %copy-start.2 = (f32[32,1024]{1,0:T(8,128)S(1)}, f32[32,1024]{1,0:T(8,128)}, u32[]{:S(2)}) copy-start(f32[32,1024]{1,0:T(8,128)} %neigh_ref.1) | copy-start | bytes 393220
  17.3 25.9 %copy-start.3 = (f32[48,32]{0,1:T(8,128)S(1)}, f32[48,32]{0,1:T(8,128)}, u32[]{:S(2)}) copy-start(f32[48,32]{0,1:T(8,128)} %param.8) | copy-start | bytes 18436
  24.5 61.3 %copy-start = (f32[48,1024]{1,0:T(8,128)S(1)}, f32[48,1024]{1,0:T(8,128)}, u32[]{:S(2)}) copy-start(f32[48,1024]{1,0:T(8,128)} %grad_ref.1) | copy-start | bytes 589828

commit v8 on v7

--- a/solution.py
+++ b/solution.py
@@ -11,6 +11,7 @@
 ROOM = 80
 SLOTS = 128
 ROW = ("y", "x")
+ACROSS = ("x", "y")
 COL = ("z", "core")
 N_ROW = 32
 N_Z = 12
@@ -54,7 +55,8 @@
     marks, counts = [], []
     for block in range(blocks):
         end = min(samples, block * 128 + 128)
-        mark = padded(owner_ref[:, block * 128 : end], -1) == (line >> 1)
+        owners = padded(owner_ref[:, block * 128 : end], -1)
+        mark = ((owners & 3) * 8 + (owners >> 2)) == (line >> 1)
         marks.append(mark)
         counts.append(
             lax.dot_general(
@@ -243,10 +245,10 @@
 def body(features, dest_feat, owner, local_row, w_self, w_neigh, grad_out):
     hid = w_self.shape[1]
     asked = requests(owner.reshape(1, -1), local_row)
-    asked = exchange(asked.reshape(N_ROW, 2, SLOTS), ROW).reshape(2 * N_ROW, SLOTS)
+    asked = exchange(asked.reshape(N_ROW, 2, SLOTS), ACROSS).reshape(2 * N_ROW, SLOTS)
     core = lax.axis_index("core")
     own = dest_feat.T
-    part = exchange(answers(asked, features, core.reshape(1)), ROW)
+    part = exchange(answers(asked, features, core.reshape(1)), ACROSS)
     agg, pre = project(part, own, w_self, w_neigh)
     pair = lax.all_gather(pre.reshape(2, DST // 2, hid), "core", axis=0, tiled=False)
     half = jnp.sum(lax.dynamic_index_in_dim(pair, core, axis=1, keepdims=False, allow_negative_indices=False), axis=0)
@@ -256,8 +258,8 @@
     half = half.reshape(3, 4, 8, 256).transpose(0, 2, 1, 3).reshape(DST // 2, hid)
     pre = lax.all_gather(half, "core", axis=0, tiled=True)
     hidden, part = gradients(pre, grad_out, own, agg)
-    total = jnp.sum(exchange(part, ROW), axis=0)
-    grads = exchange(jnp.broadcast_to(total[None], (N_ROW, 16, 128)), ROW)
+    total = jnp.sum(exchange(part, ACROSS), axis=0)
+    grads = exchange(jnp.broadcast_to(total[None], (N_ROW, 16, 128)), ACROSS)
     return (hidden, *spread(grads, hid))
 
 

time: 121 us -> 121 us (level)
  no operation moved by 1% of the time
where the time goes in v8:
time: 121 us
  blocking collectives  90.4 us (75%)
  starting transfers between devices  13 us (11%)
  Pallas kernels  7.7 us (6%)
  waiting for transfers between devices  7.23 us (6%)
  local copies, waits for them, and re-layouts  1.83 us (2%)
    all_to_all x5, blocking collectives, exchange(): return lax.all_to_all(value, axis, split_axis=0, concat_axis=0, tiled=True)  86.3 us
    all_to_all x1, starting transfers between devices, exchange(): return lax.all_to_all(value, axis, split_axis=0, concat_axis=0, tiled=True)  13 us
    all_to_all x1, waiting for transfers between devices, exchange(): return lax.all_to_all(value, axis, split_axis=0, concat_axis=0, tiled=True)  7.23 us
    pallas_call x1, Pallas kernels, answers(): pl.pallas_call(answer_kernel, in_specs=[VMEM, VMEM, VMEM, ANY], out_specs...  3.75 us
  transfers between devices with their start and end apart: 1, of which 1 were waited for; matrix products, arithmetic and copies ran while one was open for 1% of the time, Pallas kernels for 0%

profile of v8, /device:TPU:8, one launch (start us, length us, event | category | flops | bytes accessed | tf_op | source)
XLA Modules:
  0.0 120.9 jit_solution(17276349691572718609)
XLA Ops:
  0.6 2.0 %requests.1 = s32[64,128]{1,0:T(8,128)} custom-call(s32[1,1200]{1,0:T(1,128)} %bitcast.23, s32[1200]{0:T(1024)} %row_from.1), custom_call_target="tpu_custom_call" | custom-call | tf_op jit(solution)/shard_map/requests/pallas_call | solution.py:87
  2.6 13.0 %all-to-all-start = ((s32[32,2,128]{2,1,0:T(2,128)}), s32[32,2,128]{2,1,0:T(2,128)S(1)}, u32[]{:S(2)}, u32[]{:S(2)}) async-start(s32[32,2,128]{2,1,0:T(2,128)} %bitcast.22), calls=%async_computation | async-start | bytes 65536 | tf_op jit(solution)/shard_map/all_to_all | solution.py:28
  15.6 1.6 %copy.12.table_ref = f32[4096,32]{1,0:T(8,128)S(1)} copy(f32[4096,32]{0,1:T(8,128)} %param.7) | data formatting | bytes 1048576 | tf_op args[0]
  17.3 0.0 copy-start.1
  17.3 0.0 copy-start.2
  17.3 0.0 copy-start.3
  17.3 7.2 %all-to-all-done = s32[32,2,128]{2,1,0:T(2,128)S(1)} async-done(((s32[32,2,128]{2,1,0:T(2,128)}), s32[32,2,128]{2,1,0:T(2,128)S(1)}, u32[]{:S(2)}, u32[]{:S(2)}) %all-to-all-start) | async-done | bytes 32800 | tf_op jit(solution)/shard_map/all_to_all | solution.py:28
  24.6 0.1 reshape_squeeze.3.index_from
  24.7 0.0 copy-start
  24.7 3.8 %answers.1 = f32[32,16,128]{2,1,0:T(8,128)S(1)} custom-call(s32[2400]{0:T(1024)S(1)} %reshape_squeeze.3.index_from, s32[64,128]{1,0:T(8,128)S(1)} %bitcast.16, f32[4096,32]{1,0:T(8,128)S(1)} %copy.12.table_ref, s32[1]{0:T(128)} %bitcast.3.core_ref), custom_call_target="tpu_custom_call" | custom-call | tf_op jit(solution)/shard_map/answers/pallas_call | solution.py:129
  28.4 15.0 %all_to_all.30.part_ref = f32[32,16,128]{2,1,0:T(8,128)S(1)} all-to-all(f32[32,16,128]{2,1,0:T(8,128)S(1)} %answers.1), channel_id=1, replica_groups=mesh['y'=8,'x'=4,'z'=12,'core'=2] {'x','y'}, dimensions={0} | all-to-all | bytes 524288 | tf_op jit(solution)/shard_map/all_to_all | solution.py:28
  43.4 0.0 copy-done.1
  43.4 0.0 copy-done.2
  43.4 0.0 copy-done.3
  43.4 0.4 project.1
  43.8 2.1 %all_gather.6 = f32[2,2,24,1024]{3,2,1,0:T(8,128)S(1)} all-gather(f32[1,2,24,1024]{3,2,1,0:T(8,128)S(1)} %bitcast.17), channel_id=1, replica_groups=mesh['y'=8,'x'=4,'z'=12,'core'=2] {'core'}, dimensions={0}, use_global_device_ids=true | all-gather | bytes 589824 | tf_op jit(solution)/shard_map/all_gather | solution.py:253
  45.9 23.9 %all_to_all.31 = f32[12,8,256]{2,1,0:T(8,128)S(1)} all-to-all(f32[12,8,256]{2,1,0:T(8,128)S(1)} %bitcast.20), channel_id=1, replica_groups=mesh['y'=8,'x'=4,'z'=12,'core'=2] {'z'}, dimensions={0} | all-to-all | bytes 196608 | tf_op jit(solution)/shard_map/all_to_all | solution.py:28
  69.9 14.3 %all_to_all.32 = f32[12,8,256]{2,1,0:T(8,128)S(1)} all-to-all(f32[12,8,256]{2,1,0:T(8,128)S(1)} %broadcast_in_dim.4), channel_id=1, replica_groups=mesh['y'=8,'x'=4,'z'=12,'core'=2] {'z'}, dimensions={0} | all-to-all | bytes 196608 | tf_op jit(solution)/shard_map/all_to_all | solution.py:28
  84.2 1.9 %all_gather.7.pre_ref = f32[48,1024]{1,0:T(8,128)S(1)} all-gather(f32[24,1024]{1,0:T(8,128)S(1)} %bitcast.21), channel_id=1, replica_groups=mesh['y'=8,'x'=4,'z'=12,'core'=2] {'core'}, dimensions={0}, use_global_device_ids=true | all-gather | bytes 294912 | tf_op jit(solution)/shard_map/all_gather | solution.py:259
  86.1 0.0 copy-done
  86.1 0.9 gradients.1
  87.0 16.9 %all_to_all.33 = f32[32,16,128]{2,1,0:T(8,128)S(1)} all-to-all(f32[32,16,128]{2,1,0:T(8,128)S(1)} %get-tuple-element.12), channel_id=1, replica_groups=mesh['y'=8,'x'=4,'z'=12,'core'=2] {'x','y'}, dimensions={0} | all-to-all | bytes 524288 | tf_op jit(solution)/shard_map/all_to_all | solution.py:28
  104.0 16.2 %all_to_all.34.block_ref = f32[32,16,128]{2,1,0:T(8,128)S(1)} all-to-all(f32[32,16,128]{2,1,0:T(8,128)S(1)} %broadcast_in_dim.5), channel_id=1, replica_groups=mesh['y'=8,'x'=4,'z'=12,'core'=2] {'x','y'}, dimensions={0} | all-to-all | bytes 524288 | tf_op jit(solution)/shard_map/all_to_all | solution.py:28
  120.2 0.7 spread.1
  (6 shorter events, 0.1 us)
Async XLA Ops:
  2.6 21.9 %all-to-all-start = ((s32[32,2,128]{2,1,0:T(2,128)}), s32[32,2,128]{2,1,0:T(2,128)S(1)}, u32[]{:S(2)}, u32[]{:S(2)}) async-start(s32[32,2,128]{2,1,0:T(2,128)} %bitcast.22), calls=%async_computation | async-start | bytes 65536 | tf_op jit(solution)/shard_map/all_to_all | solution.py:28
  17.3 26.2 %copy-start.1 = (f32[32,1024]{1,0:T(8,128)S(1)}, f32[32,1024]{1,0:T(8,128)}, u32[]{:S(2)}) copy-start(f32[32,1024]{1,0:T(8,128)} %self_ref.1) | copy-start | bytes 393220
  17.3 26.2 %copy-start.2 = (f32[32,1024]{1,0:T(8,128)S(1)}, f32[32,1024]{1,0:T(8,128)}, u32[]{:S(2)}) copy-start(f32[32,1024]{1,0:T(8,128)} %neigh_ref.1) | copy-start | bytes 393220
  17.3 26.1 %copy-start.3 = (f32[48,32]{0,1:T(8,128)S(1)}, f32[48,32]{0,1:T(8,128)}, u32[]{:S(2)}) copy-start(f32[48,32]{0,1:T(8,128)} %param.8) | copy-start | bytes 18436
  24.7 61.4 %copy-start = (f32[48,1024]{1,0:T(8,128)S(1)}, f32[48,1024]{1,0:T(8,128)}, u32[]{:S(2)}) copy-start(f32[48,1024]{1,0:T(8,128)} %grad_ref.1) | copy-start | bytes 589828

commit v9 on v7

--- a/solution.py
+++ b/solution.py
@@ -219,7 +219,9 @@
     )(pre, grad_out, own, part)
 
 
-def spread_kernel(block_ref, self_ref, neigh_ref):
+def spread_kernel(block_ref, hidden_ref, self_ref, neigh_ref, hidden_to, sem):
+    store = pltpu.make_async_copy(hidden_ref, hidden_to, sem)
+    store.start()
     lanes = self_ref.shape[1] // 128
     for at, out_ref in ((0, self_ref), (1, neigh_ref)):
         for line in range(2):
@@ -227,17 +229,20 @@
                 out_ref[line * 16 : line * 16 + 16, lane * 128 : lane * 128 + 128] = block_ref[
                     (2 * at + line) * lanes + lane
                 ]
-
-
-def spread(blocks, hid):
+    store.wait()
+
+
+def spread(blocks, hidden):
+    grad = jax.ShapeDtypeStruct((32, hidden.shape[1]), jnp.float32)
     return pl.pallas_call(
         spread_kernel,
-        in_specs=[VMEM],
-        out_specs=[VMEM] * 2,
-        out_shape=[jax.ShapeDtypeStruct((32, hid), jnp.float32)] * 2,
+        in_specs=[VMEM] * 2,
+        out_specs=[VMEM, VMEM, HBM],
+        out_shape=[grad, grad, jax.ShapeDtypeStruct(hidden.shape, jnp.float32)],
+        scratch_shapes=[pltpu.SemaphoreType.DMA],
         compiler_params=SMALL,
         name="spread",
-    )(blocks)
+    )(blocks, hidden)
 
 
 def body(features, dest_feat, owner, local_row, w_self, w_neigh, grad_out):
@@ -258,7 +263,8 @@
     hidden, part = gradients(pre, grad_out, own, agg)
     total = jnp.sum(exchange(part, ROW), axis=0)
     grads = exchange(jnp.broadcast_to(total[None], (N_ROW, 16, 128)), ROW)
-    return (hidden, *spread(grads, hid))
+    grad_self, grad_neigh, hidden = spread(grads, hidden)
+    return (hidden, grad_self, grad_neigh)
 
 
 def solution(mesh):

time: 121 us -> 121 us (level)
  no operation moved by 1% of the time
where the time goes in v9:
time: 121 us
  blocking collectives  90 us (74%)
  starting transfers between devices  13 us (11%)
  Pallas kernels  7.87 us (7%)
  waiting for transfers between devices  7.07 us (6%)
  local copies, waits for them, and re-layouts  1.83 us (2%)
    all_to_all x5, blocking collectives, exchange(): return lax.all_to_all(value, axis, split_axis=0, concat_axis=0, tiled=True)  85.9 us
    all_to_all x1, starting transfers between devices, exchange(): return lax.all_to_all(value, axis, split_axis=0, concat_axis=0, tiled=True)  13 us
    all_to_all x1, waiting for transfers between devices, exchange(): return lax.all_to_all(value, axis, split_axis=0, concat_axis=0, tiled=True)  7.07 us
    pallas_call x1, Pallas kernels, answers(): pl.pallas_call(answer_kernel, in_specs=[VMEM, VMEM, VMEM, ANY], out_specs...  3.75 us
  transfers between devices with their start and end apart: 1, of which 1 were waited for; matrix products, arithmetic and copies ran while one was open for 1% of the time, Pallas kernels for 0%

profile of v9, /device:TPU:8, one launch (start us, length us, event | category | flops | bytes accessed | tf_op | source)
XLA Modules:
  0.0 120.6 jit_solution(9520767294921440667)
XLA Ops:
  0.6 2.0 %requests.1 = s32[64,128]{1,0:T(8,128)} custom-call(s32[1,1200]{1,0:T(1,128)} %bitcast.23, s32[1200]{0:T(1024)} %row_from.1), custom_call_target="tpu_custom_call" | custom-call | tf_op jit(solution)/shard_map/requests/pallas_call | solution.py:85
  2.6 13.0 %all-to-all-start = ((s32[32,2,128]{2,1,0:T(2,128)}), s32[32,2,128]{2,1,0:T(2,128)S(1)}, u32[]{:S(2)}, u32[]{:S(2)}) async-start(s32[32,2,128]{2,1,0:T(2,128)} %bitcast.22), calls=%async_computation | async-start | bytes 65536 | tf_op jit(solution)/shard_map/all_to_all | solution.py:27
  15.6 1.6 %copy.12.table_ref = f32[4096,32]{1,0:T(8,128)S(1)} copy(f32[4096,32]{0,1:T(8,128)} %param.7) | data formatting | bytes 1048576 | tf_op args[0]
  17.3 0.0 copy-start.1
  17.3 0.0 copy-start.2
  17.3 0.0 copy-start.3
  17.3 7.1 %all-to-all-done = s32[32,2,128]{2,1,0:T(2,128)S(1)} async-done(((s32[32,2,128]{2,1,0:T(2,128)}), s32[32,2,128]{2,1,0:T(2,128)S(1)}, u32[]{:S(2)}, u32[]{:S(2)}) %all-to-all-start) | async-done | bytes 32800 | tf_op jit(solution)/shard_map/all_to_all | solution.py:27
  24.4 0.1 reshape_squeeze.3.index_from
  24.5 0.0 copy-start
  24.6 3.7 %answers.1 = f32[32,16,128]{2,1,0:T(8,128)S(1)} custom-call(s32[2400]{0:T(1024)S(1)} %reshape_squeeze.3.index_from, s32[64,128]{1,0:T(8,128)S(1)} %bitcast.16, f32[4096,32]{1,0:T(8,128)S(1)} %copy.12.table_ref, s32[1]{0:T(128)} %bitcast.3.core_ref), custom_call_target="tpu_custom_call" | custom-call | tf_op jit(solution)/shard_map/answers/pallas_call | solution.py:127
  28.3 14.9 %all_to_all.30.part_ref = f32[32,16,128]{2,1,0:T(8,128)S(1)} all-to-all(f32[32,16,128]{2,1,0:T(8,128)S(1)} %answers.1), channel_id=1, replica_groups=mesh['y'=8,'x'=4,'z'=12,'core'=2] {'y','x'}, dimensions={0} | all-to-all | bytes 524288 | tf_op jit(solution)/shard_map/all_to_all | solution.py:27
  43.2 0.0 copy-done.1
  43.2 0.0 copy-done.2
  43.2 0.0 copy-done.3
  43.2 0.4 project.1
  43.6 2.1 %all_gather.6 = f32[2,2,24,1024]{3,2,1,0:T(8,128)S(1)} all-gather(f32[1,2,24,1024]{3,2,1,0:T(8,128)S(1)} %bitcast.17), channel_id=1, replica_groups=mesh['y'=8,'x'=4,'z'=12,'core'=2] {'core'}, dimensions={0}, use_global_device_ids=true | all-gather | bytes 589824 | tf_op jit(solution)/shard_map/all_gather | solution.py:256
  45.7 24.0 %all_to_all.31 = f32[12,8,256]{2,1,0:T(8,128)S(1)} all-to-all(f32[12,8,256]{2,1,0:T(8,128)S(1)} %bitcast.20), channel_id=1, replica_groups=mesh['y'=8,'x'=4,'z'=12,'core'=2] {'z'}, dimensions={0} | all-to-all | bytes 196608 | tf_op jit(solution)/shard_map/all_to_all | solution.py:27
  69.7 14.3 %all_to_all.32 = f32[12,8,256]{2,1,0:T(8,128)S(1)} all-to-all(f32[12,8,256]{2,1,0:T(8,128)S(1)} %broadcast_in_dim.4), channel_id=1, replica_groups=mesh['y'=8,'x'=4,'z'=12,'core'=2] {'z'}, dimensions={0} | all-to-all | bytes 196608 | tf_op jit(solution)/shard_map/all_to_all | solution.py:27
  84.0 1.9 %all_gather.7.pre_ref = f32[48,1024]{1,0:T(8,128)S(1)} all-gather(f32[24,1024]{1,0:T(8,128)S(1)} %bitcast.21), channel_id=1, replica_groups=mesh['y'=8,'x'=4,'z'=12,'core'=2] {'core'}, dimensions={0}, use_global_device_ids=true | all-gather | bytes 294912 | tf_op jit(solution)/shard_map/all_gather | solution.py:262
  85.9 0.0 copy-done
  85.9 0.4 gradients.1
  86.3 16.9 %all_to_all.33 = f32[32,16,128]{2,1,0:T(8,128)S(1)} all-to-all(f32[32,16,128]{2,1,0:T(8,128)S(1)} %get-tuple-element.12), channel_id=1, replica_groups=mesh['y'=8,'x'=4,'z'=12,'core'=2] {'y','x'}, dimensions={0} | all-to-all | bytes 524288 | tf_op jit(solution)/shard_map/all_to_all | solution.py:27
  103.2 15.9 %all_to_all.34.block_ref = f32[32,16,128]{2,1,0:T(8,128)S(1)} all-to-all(f32[32,16,128]{2,1,0:T(8,128)S(1)} %broadcast_in_dim.5), channel_id=1, replica_groups=mesh['y'=8,'x'=4,'z'=12,'core'=2] {'y','x'}, dimensions={0} | all-to-all | bytes 524288 | tf_op jit(solution)/shard_map/all_to_all | solution.py:27
  119.2 1.4 %spread.1 = (f32[32,1024]{1,0:T(8,128)}, f32[32,1024]{1,0:T(8,128)}, f32[48,1024]{1,0:T(8,128)}) custom-call(f32[32,16,128]{2,1,0:T(8,128)S(1)} %all_to_all.34.block_ref, f32[48,1024]{1,0:T(8,128)S(1)} %get-tuple-element.13.hidden_ref), custom_call_target="tpu_custom_call" | custom-call | tf_op jit(solution)/shard_map/spread/pallas_call | solution.py:237
  (6 shorter events, 0.1 us)
Async XLA Ops:
  2.6 21.8 %all-to-all-start = ((s32[32,2,128]{2,1,0:T(2,128)}), s32[32,2,128]{2,1,0:T(2,128)S(1)}, u32[]{:S(2)}, u32[]{:S(2)}) async-start(s32[32,2,128]{2,1,0:T(2,128)} %bitcast.22), calls=%async_computation | async-start | bytes 65536 | tf_op jit(solution)/shard_map/all_to_all | solution.py:27
  17.3 25.9 %copy-start.1 = (f32[32,1024]{1,0:T(8,128)S(1)}, f32[32,1024]{1,0:T(8,128)}, u32[]{:S(2)}) copy-start(f32[32,1024]{1,0:T(8,128)} %self_ref.1) | copy-start | bytes 393220
  17.3 25.9 %copy-start.2 = (f32[32,1024]{1,0:T(8,128)S(1)}, f32[32,1024]{1,0:T(8,128)}, u32[]{:S(2)}) copy-start(f32[32,1024]{1,0:T(8,128)} %neigh_ref.1) | copy-start | bytes 393220
  17.3 25.9 %copy-start.3 = (f32[48,32]{0,1:T(8,128)S(1)}, f32[48,32]{0,1:T(8,128)}, u32[]{:S(2)}) copy-start(f32[48,32]{0,1:T(8,128)} %param.8) | copy-start | bytes 18436
  24.5 61.4 %copy-start = (f32[48,1024]{1,0:T(8,128)S(1)}, f32[48,1024]{1,0:T(8,128)}, u32[]{:S(2)}) copy-start(f32[48,1024]{1,0:T(8,128)} %grad_ref.1) | copy-start | bytes 589828

commit v10 on v7

--- a/solution.py
+++ b/solution.py
@@ -10,6 +10,7 @@
 CAP = 75
 ROOM = 80
 SLOTS = 128
+GROUP = 8
 ROW = ("y", "x")
 COL = ("z", "core")
 N_ROW = 32
@@ -106,19 +107,23 @@
         place_ref[r] = jnp.where(dest == line, 1.0, 0.0).astype(jnp.bfloat16)
         held_ref[r, ROOM - 8 :, :] = jnp.zeros((8, width), jnp.float32)
     load.wait()
-
-    def fetch(r, carry):
-        for s in range(CAP):
-            held_ref[r, s : s + 1, :] = table_ref[pl.ds(index_ref[r * CAP + s], 1), :]
-        return carry
-
-    lax.fori_loop(0, N_ROW, fetch, 0)
     gap = jnp.zeros((16, 128 - 3 * width), jnp.float32)
-    for r in range(N_ROW):
+
+    def fetch(r, s):
+        held_ref[r, s : s + 1, :] = table_ref[pl.ds(index_ref[r * CAP + s], 1), :]
+
+    def reply(r):
         lead, rest = split(held_ref[r])
         total = jnp.dot(place_ref[r], jnp.concatenate([lead, rest], axis=1), preferred_element_type=jnp.float32)
         total = total[:, :width] + total[:, width:]
         out_ref[r] = jnp.concatenate([total[:16], total[16:32], total[32:], gap], axis=1)
+
+    for r in range(N_ROW + GROUP):
+        if r >= GROUP:
+            reply(r - GROUP)
+        if r < N_ROW:
+            for s in range(CAP):
+                fetch(r, s)
 
 
 def answers(asked, table, core):

time: 121 us -> 120 us (level)
  no operation moved by 1% of the time
where the time goes in v10:
time: 120 us
  blocking collectives  90 us (75%)
  starting transfers between devices  13 us (11%)
  waiting for transfers between devices  7.07 us (6%)
  Pallas kernels  7 us (6%)
  local copies, waits for them, and re-layouts  1.83 us (2%)
    all_to_all x5, blocking collectives, exchange(): return lax.all_to_all(value, axis, split_axis=0, concat_axis=0, tiled=True)  85.9 us
    all_to_all x1, starting transfers between devices, exchange(): return lax.all_to_all(value, axis, split_axis=0, concat_axis=0, tiled=True)  13 us
    all_to_all x1, waiting for transfers between devices, exchange(): return lax.all_to_all(value, axis, split_axis=0, concat_axis=0, tiled=True)  7.07 us
    pallas_call x1, Pallas kernels, answers(): pl.pallas_call(answer_kernel, in_specs=[VMEM, VMEM, VMEM, ANY], out_specs...  3.05 us
  transfers between devices with their start and end apart: 1, of which 1 were waited for; matrix products, arithmetic and copies ran while one was open for 1% of the time, Pallas kernels for 0%

profile of v10, /device:TPU:8, one launch (start us, length us, event | category | flops | bytes accessed | tf_op | source)
XLA Modules:
  0.0 119.7 jit_solution(11342081642932021483)
XLA Ops:
  0.6 2.0 %requests.1 = s32[64,128]{1,0:T(8,128)} custom-call(s32[1,1200]{1,0:T(1,128)} %bitcast.23, s32[1200]{0:T(1024)} %row_from.1), custom_call_target="tpu_custom_call" | custom-call | tf_op jit(solution)/shard_map/requests/pallas_call | solution.py:86
  2.6 13.0 %all-to-all-start = ((s32[32,2,128]{2,1,0:T(2,128)}), s32[32,2,128]{2,1,0:T(2,128)S(1)}, u32[]{:S(2)}, u32[]{:S(2)}) async-start(s32[32,2,128]{2,1,0:T(2,128)} %bitcast.22), calls=%async_computation | async-start | bytes 65536 | tf_op jit(solution)/shard_map/all_to_all | solution.py:28
  15.6 1.6 %copy.12.table_ref = f32[4096,32]{1,0:T(8,128)S(1)} copy(f32[4096,32]{0,1:T(8,128)} %param.7) | data formatting | bytes 1048576 | tf_op args[0]
  17.3 0.0 copy-start.1
  17.3 0.0 copy-start.2
  17.3 0.0 copy-start.3
  17.3 7.1 %all-to-all-done = s32[32,2,128]{2,1,0:T(2,128)S(1)} async-done(((s32[32,2,128]{2,1,0:T(2,128)}), s32[32,2,128]{2,1,0:T(2,128)S(1)}, u32[]{:S(2)}, u32[]{:S(2)}) %all-to-all-start) | async-done | bytes 32800 | tf_op jit(solution)/shard_map/all_to_all | solution.py:28
  24.4 0.1 reshape_squeeze.3.index_from
  24.5 0.0 copy-start
  24.6 3.0 %answers.1 = f32[32,16,128]{2,1,0:T(8,128)S(1)} custom-call(s32[2400]{0:T(1024)S(1)} %reshape_squeeze.3.index_from, s32[64,128]{1,0:T(8,128)S(1)} %bitcast.16, f32[4096,32]{1,0:T(8,128)S(1)} %copy.12.table_ref, s32[1]{0:T(128)} %bitcast.3.core_ref), custom_call_target="tpu_custom_call" | custom-call | tf_op jit(solution)/shard_map/answers/pallas_call | solution.py:132
  27.6 14.9 %all_to_all.30.part_ref = f32[32,16,128]{2,1,0:T(8,128)S(1)} all-to-all(f32[32,16,128]{2,1,0:T(8,128)S(1)} %answers.1), channel_id=1, replica_groups=mesh['y'=8,'x'=4,'z'=12,'core'=2] {'y','x'}, dimensions={0} | all-to-all | bytes 524288 | tf_op jit(solution)/shard_map/all_to_all | solution.py:28
  42.5 0.0 copy-done.1
  42.5 0.0 copy-done.2
  42.5 0.0 copy-done.3
  42.5 0.4 project.1
  42.9 2.1 %all_gather.6 = f32[2,2,24,1024]{3,2,1,0:T(8,128)S(1)} all-gather(f32[1,2,24,1024]{3,2,1,0:T(8,128)S(1)} %bitcast.17), channel_id=1, replica_groups=mesh['y'=8,'x'=4,'z'=12,'core'=2] {'core'}, dimensions={0}, use_global_device_ids=true | all-gather | bytes 589824 | tf_op jit(solution)/shard_map/all_gather | solution.py:256
  45.0 24.0 %all_to_all.31 = f32[12,8,256]{2,1,0:T(8,128)S(1)} all-to-all(f32[12,8,256]{2,1,0:T(8,128)S(1)} %bitcast.20), channel_id=1, replica_groups=mesh['y'=8,'x'=4,'z'=12,'core'=2] {'z'}, dimensions={0} | all-to-all | bytes 196608 | tf_op jit(solution)/shard_map/all_to_all | solution.py:28
  69.0 14.3 %all_to_all.32 = f32[12,8,256]{2,1,0:T(8,128)S(1)} all-to-all(f32[12,8,256]{2,1,0:T(8,128)S(1)} %broadcast_in_dim.4), channel_id=1, replica_groups=mesh['y'=8,'x'=4,'z'=12,'core'=2] {'z'}, dimensions={0} | all-to-all | bytes 196608 | tf_op jit(solution)/shard_map/all_to_all | solution.py:28
  83.3 1.9 %all_gather.7.pre_ref = f32[48,1024]{1,0:T(8,128)S(1)} all-gather(f32[24,1024]{1,0:T(8,128)S(1)} %bitcast.21), channel_id=1, replica_groups=mesh['y'=8,'x'=4,'z'=12,'core'=2] {'core'}, dimensions={0}, use_global_device_ids=true | all-gather | bytes 294912 | tf_op jit(solution)/shard_map/all_gather | solution.py:262
  85.2 0.0 copy-done
  85.2 0.9 gradients.1
  86.1 16.9 %all_to_all.33 = f32[32,16,128]{2,1,0:T(8,128)S(1)} all-to-all(f32[32,16,128]{2,1,0:T(8,128)S(1)} %get-tuple-element.12), channel_id=1, replica_groups=mesh['y'=8,'x'=4,'z'=12,'core'=2] {'y','x'}, dimensions={0} | all-to-all | bytes 524288 | tf_op jit(solution)/shard_map/all_to_all | solution.py:28
  103.0 15.9 %all_to_all.34.block_ref = f32[32,16,128]{2,1,0:T(8,128)S(1)} all-to-all(f32[32,16,128]{2,1,0:T(8,128)S(1)} %broadcast_in_dim.5), channel_id=1, replica_groups=mesh['y'=8,'x'=4,'z'=12,'core'=2] {'y','x'}, dimensions={0} | all-to-all | bytes 524288 | tf_op jit(solution)/shard_map/all_to_all | solution.py:28
  118.9 0.7 spread.1
  (6 shorter events, 0.1 us)
Async XLA Ops:
  2.6 21.8 %all-to-all-start = ((s32[32,2,128]{2,1,0:T(2,128)}), s32[32,2,128]{2,1,0:T(2,128)S(1)}, u32[]{:S(2)}, u32[]{:S(2)}) async-start(s32[32,2,128]{2,1,0:T(2,128)} %bitcast.22), calls=%async_computation | async-start | bytes 65536 | tf_op jit(solution)/shard_map/all_to_all | solution.py:28
  17.3 25.2 %copy-start.1 = (f32[32,1024]{1,0:T(8,128)S(1)}, f32[32,1024]{1,0:T(8,128)}, u32[]{:S(2)}) copy-start(f32[32,1024]{1,0:T(8,128)} %self_ref.1) | copy-start | bytes 393220
  17.3 25.2 %copy-start.2 = (f32[32,1024]{1,0:T(8,128)S(1)}, f32[32,1024]{1,0:T(8,128)}, u32[]{:S(2)}) copy-start(f32[32,1024]{1,0:T(8,128)} %neigh_ref.1) | copy-start | bytes 393220
  17.3 25.2 %copy-start.3 = (f32[48,32]{0,1:T(8,128)S(1)}, f32[48,32]{0,1:T(8,128)}, u32[]{:S(2)}) copy-start(f32[48,32]{0,1:T(8,128)} %param.8) | copy-start | bytes 18436
  24.5 60.7 %copy-start = (f32[48,1024]{1,0:T(8,128)S(1)}, f32[48,1024]{1,0:T(8,128)}, u32[]{:S(2)}) copy-start(f32[48,1024]{1,0:T(8,128)} %grad_ref.1) | copy-start | bytes 589828

commit v11 on v10

--- a/solution.py
+++ b/solution.py
@@ -12,6 +12,7 @@
 SLOTS = 128
 GROUP = 8
 ROW = ("y", "x")
+ACROSS = ("x", "y")
 COL = ("z", "core")
 N_ROW = 32
 N_Z = 12
@@ -55,7 +56,8 @@
     marks, counts = [], []
     for block in range(blocks):
         end = min(samples, block * 128 + 128)
-        mark = padded(owner_ref[:, block * 128 : end], -1) == (line >> 1)
+        owners = padded(owner_ref[:, block * 128 : end], -1)
+        mark = ((owners & 3) * 8 + (owners >> 2)) == (line >> 1)
         marks.append(mark)
         counts.append(
             lax.dot_general(
@@ -248,10 +250,10 @@
 def body(features, dest_feat, owner, local_row, w_self, w_neigh, grad_out):
     hid = w_self.shape[1]
     asked = requests(owner.reshape(1, -1), local_row)
-    asked = exchange(asked.reshape(N_ROW, 2, SLOTS), ROW).reshape(2 * N_ROW, SLOTS)
+    asked = exchange(asked.reshape(N_ROW, 2, SLOTS), ACROSS).reshape(2 * N_ROW, SLOTS)
     core = lax.axis_index("core")
     own = dest_feat.T
-    part = exchange(answers(asked, features, core.reshape(1)), ROW)
+    part = exchange(answers(asked, features, core.reshape(1)), ACROSS)
     agg, pre = project(part, own, w_self, w_neigh)
     pair = lax.all_gather(pre.reshape(2, DST // 2, hid), "core", axis=0, tiled=False)
     half = jnp.sum(lax.dynamic_index_in_dim(pair, core, axis=1, keepdims=False, allow_negative_indices=False), axis=0)

time: 120 us -> 120 us (level)
  no operation moved by 1% of the time
where the time goes in v11:
time: 120 us
  blocking collectives  89.9 us (75%)
  starting transfers between devices  13 us (11%)
  waiting for transfers between devices  7.23 us (6%)
  Pallas kernels  7.01 us (6%)
  local copies, waits for them, and re-layouts  1.83 us (2%)
    all_to_all x5, blocking collectives, exchange(): return lax.all_to_all(value, axis, split_axis=0, concat_axis=0, tiled=True)  85.9 us
    all_to_all x1, starting transfers between devices, exchange(): return lax.all_to_all(value, axis, split_axis=0, concat_axis=0, tiled=True)  13 us
    all_to_all x1, waiting for transfers between devices, exchange(): return lax.all_to_all(value, axis, split_axis=0, concat_axis=0, tiled=True)  7.23 us
    pallas_call x1, Pallas kernels, answers(): pl.pallas_call(answer_kernel, in_specs=[VMEM, VMEM, VMEM, ANY], out_specs...  3.06 us
  transfers between devices with their start and end apart: 1, of which 1 were waited for; matrix products, arithmetic and copies ran while one was open for 1% of the time, Pallas kernels for 0%

profile of v11, /device:TPU:8, one launch (start us, length us, event | category | flops | bytes accessed | tf_op | source)
XLA Modules:
  0.0 119.8 jit_solution(16332885681584008371)
XLA Ops:
  0.6 2.0 %requests.1 = s32[64,128]{1,0:T(8,128)} custom-call(s32[1,1200]{1,0:T(1,128)} %bitcast.23, s32[1200]{0:T(1024)} %row_from.1), custom_call_target="tpu_custom_call" | custom-call | tf_op jit(solution)/shard_map/requests/pallas_call | solution.py:88
  2.6 13.0 %all-to-all-start = ((s32[32,2,128]{2,1,0:T(2,128)}), s32[32,2,128]{2,1,0:T(2,128)S(1)}, u32[]{:S(2)}, u32[]{:S(2)}) async-start(s32[32,2,128]{2,1,0:T(2,128)} %bitcast.22), calls=%async_computation | async-start | bytes 65536 | tf_op jit(solution)/shard_map/all_to_all | solution.py:29
  15.6 1.6 %copy.12.table_ref = f32[4096,32]{1,0:T(8,128)S(1)} copy(f32[4096,32]{0,1:T(8,128)} %param.7) | data formatting | bytes 1048576 | tf_op args[0]
  17.3 0.0 copy-start.1
  17.3 0.0 copy-start.2
  17.3 0.0 copy-start.3
  17.3 7.2 %all-to-all-done = s32[32,2,128]{2,1,0:T(2,128)S(1)} async-done(((s32[32,2,128]{2,1,0:T(2,128)}), s32[32,2,128]{2,1,0:T(2,128)S(1)}, u32[]{:S(2)}, u32[]{:S(2)}) %all-to-all-start) | async-done | bytes 32800 | tf_op jit(solution)/shard_map/all_to_all | solution.py:29
  24.6 0.1 reshape_squeeze.3.index_from
  24.7 0.0 copy-start
  24.7 3.1 %answers.1 = f32[32,16,128]{2,1,0:T(8,128)S(1)} custom-call(s32[2400]{0:T(1024)S(1)} %reshape_squeeze.3.index_from, s32[64,128]{1,0:T(8,128)S(1)} %bitcast.16, f32[4096,32]{1,0:T(8,128)S(1)} %copy.12.table_ref, s32[1]{0:T(128)} %bitcast.3.core_ref), custom_call_target="tpu_custom_call" | custom-call | tf_op jit(solution)/shard_map/answers/pallas_call | solution.py:134
  27.8 15.0 %all_to_all.30.part_ref = f32[32,16,128]{2,1,0:T(8,128)S(1)} all-to-all(f32[32,16,128]{2,1,0:T(8,128)S(1)} %answers.1), channel_id=1, replica_groups=mesh['y'=8,'x'=4,'z'=12,'core'=2] {'x','y'}, dimensions={0} | all-to-all | bytes 524288 | tf_op jit(solution)/shard_map/all_to_all | solution.py:29
  42.7 0.0 copy-done.1
  42.7 0.0 copy-done.2
  42.7 0.0 copy-done.3
  42.7 0.4 project.1
  43.1 2.1 %all_gather.6 = f32[2,2,24,1024]{3,2,1,0:T(8,128)S(1)} all-gather(f32[1,2,24,1024]{3,2,1,0:T(8,128)S(1)} %bitcast.17), channel_id=1, replica_groups=mesh['y'=8,'x'=4,'z'=12,'core'=2] {'core'}, dimensions={0}, use_global_device_ids=true | all-gather | bytes 589824 | tf_op jit(solution)/shard_map/all_gather | solution.py:258
  45.2 23.9 %all_to_all.31 = f32[12,8,256]{2,1,0:T(8,128)S(1)} all-to-all(f32[12,8,256]{2,1,0:T(8,128)S(1)} %bitcast.20), channel_id=1, replica_groups=mesh['y'=8,'x'=4,'z'=12,'core'=2] {'z'}, dimensions={0} | all-to-all | bytes 196608 | tf_op jit(solution)/shard_map/all_to_all | solution.py:29
  69.2 14.3 %all_to_all.32 = f32[12,8,256]{2,1,0:T(8,128)S(1)} all-to-all(f32[12,8,256]{2,1,0:T(8,128)S(1)} %broadcast_in_dim.4), channel_id=1, replica_groups=mesh['y'=8,'x'=4,'z'=12,'core'=2] {'z'}, dimensions={0} | all-to-all | bytes 196608 | tf_op jit(solution)/shard_map/all_to_all | solution.py:29
  83.5 1.9 %all_gather.7.pre_ref = f32[48,1024]{1,0:T(8,128)S(1)} all-gather(f32[24,1024]{1,0:T(8,128)S(1)} %bitcast.21), channel_id=1, replica_groups=mesh['y'=8,'x'=4,'z'=12,'core'=2] {'core'}, dimensions={0}, use_global_device_ids=true | all-gather | bytes 294912 | tf_op jit(solution)/shard_map/all_gather | solution.py:264
  85.4 0.0 copy-done
  85.4 0.9 gradients.1
  86.3 16.8 %all_to_all.33 = f32[32,16,128]{2,1,0:T(8,128)S(1)} all-to-all(f32[32,16,128]{2,1,0:T(8,128)S(1)} %get-tuple-element.12), channel_id=1, replica_groups=mesh['y'=8,'x'=4,'z'=12,'core'=2] {'y','x'}, dimensions={0} | all-to-all | bytes 524288 | tf_op jit(solution)/shard_map/all_to_all | solution.py:29
  103.2 15.9 %all_to_all.34.block_ref = f32[32,16,128]{2,1,0:T(8,128)S(1)} all-to-all(f32[32,16,128]{2,1,0:T(8,128)S(1)} %broadcast_in_dim.5), channel_id=1, replica_groups=mesh['y'=8,'x'=4,'z'=12,'core'=2] {'y','x'}, dimensions={0} | all-to-all | bytes 524288 | tf_op jit(solution)/shard_map/all_to_all | solution.py:29
  119.1 0.7 spread.1
  (6 shorter events, 0.1 us)
Async XLA Ops:
  2.6 21.9 %all-to-all-start = ((s32[32,2,128]{2,1,0:T(2,128)}), s32[32,2,128]{2,1,0:T(2,128)S(1)}, u32[]{:S(2)}, u32[]{:S(2)}) async-start(s32[32,2,128]{2,1,0:T(2,128)} %bitcast.22), calls=%async_computation | async-start | bytes 65536 | tf_op jit(solution)/shard_map/all_to_all | solution.py:29
  17.3 25.5 %copy-start.1 = (f32[32,1024]{1,0:T(8,128)S(1)}, f32[32,1024]{1,0:T(8,128)}, u32[]{:S(2)}) copy-start(f32[32,1024]{1,0:T(8,128)} %self_ref.1) | copy-start | bytes 393220
  17.3 25.5 %copy-start.2 = (f32[32,1024]{1,0:T(8,128)S(1)}, f32[32,1024]{1,0:T(8,128)}, u32[]{:S(2)}) copy-start(f32[32,1024]{1,0:T(8,128)} %neigh_ref.1) | copy-start | bytes 393220
  17.3 25.4 %copy-start.3 = (f32[48,32]{0,1:T(8,128)S(1)}, f32[48,32]{0,1:T(8,128)}, u32[]{:S(2)}) copy-start(f32[48,32]{0,1:T(8,128)} %param.8) | copy-start | bytes 18436
  24.7 60.7 %copy-start = (f32[48,1024]{1,0:T(8,128)S(1)}, f32[48,1024]{1,0:T(8,128)}, u32[]{:S(2)}) copy-start(f32[48,1024]{1,0:T(8,128)} %grad_ref.1) | copy-start | bytes 589828

commit v12 on v10

--- a/solution.py
+++ b/solution.py
@@ -10,7 +10,7 @@
 CAP = 75
 ROOM = 80
 SLOTS = 128
-GROUP = 8
+GROUP = 4
 ROW = ("y", "x")
 COL = ("z", "core")
 N_ROW = 32

time: 120 us -> 120 us (level)
  no operation moved by 1% of the time
where the time goes in v12:
time: 120 us
  blocking collectives  89.9 us (75%)
  starting transfers between devices  13 us (11%)
  waiting for transfers between devices  7.07 us (6%)
  Pallas kernels  6.99 us (6%)
  local copies, waits for them, and re-layouts  1.83 us (2%)
    all_to_all x5, blocking collectives, exchange(): return lax.all_to_all(value, axis, split_axis=0, concat_axis=0, tiled=True)  85.9 us
    all_to_all x1, starting transfers between devices, exchange(): return lax.all_to_all(value, axis, split_axis=0, concat_axis=0, tiled=True)  13 us
    all_to_all x1, waiting for transfers between devices, exchange(): return lax.all_to_all(value, axis, split_axis=0, concat_axis=0, tiled=True)  7.07 us
    pallas_call x1, Pallas kernels, answers(): pl.pallas_call(answer_kernel, in_specs=[VMEM, VMEM, VMEM, ANY], out_specs...  3.04 us
  transfers between devices with their start and end apart: 1, of which 1 were waited for; matrix products, arithmetic and copies ran while one was open for 1% of the time, Pallas kernels for 0%

profile of v12, /device:TPU:8, one launch (start us, length us, event | category | flops | bytes accessed | tf_op | source)
XLA Modules:
  0.0 119.6 jit_solution(11342081642932021483)
XLA Ops:
  0.6 2.0 %requests.1 = s32[64,128]{1,0:T(8,128)} custom-call(s32[1,1200]{1,0:T(1,128)} %bitcast.23, s32[1200]{0:T(1024)} %row_from.1), custom_call_target="tpu_custom_call" | custom-call | tf_op jit(solution)/shard_map/requests/pallas_call | solution.py:86
  2.6 13.0 %all-to-all-start = ((s32[32,2,128]{2,1,0:T(2,128)}), s32[32,2,128]{2,1,0:T(2,128)S(1)}, u32[]{:S(2)}, u32[]{:S(2)}) async-start(s32[32,2,128]{2,1,0:T(2,128)} %bitcast.22), calls=%async_computation | async-start | bytes 65536 | tf_op jit(solution)/shard_map/all_to_all | solution.py:28
  15.6 1.6 %copy.12.table_ref = f32[4096,32]{1,0:T(8,128)S(1)} copy(f32[4096,32]{0,1:T(8,128)} %param.7) | data formatting | bytes 1048576 | tf_op args[0]
  17.3 0.0 copy-start.1
  17.3 0.0 copy-start.2
  17.3 0.0 copy-start.3
  17.3 7.1 %all-to-all-done = s32[32,2,128]{2,1,0:T(2,128)S(1)} async-done(((s32[32,2,128]{2,1,0:T(2,128)}), s32[32,2,128]{2,1,0:T(2,128)S(1)}, u32[]{:S(2)}, u32[]{:S(2)}) %all-to-all-start) | async-done | bytes 32800 | tf_op jit(solution)/shard_map/all_to_all | solution.py:28
  24.4 0.1 reshape_squeeze.3.index_from
  24.5 0.0 copy-start
  24.6 3.0 %answers.1 = f32[32,16,128]{2,1,0:T(8,128)S(1)} custom-call(s32[2400]{0:T(1024)S(1)} %reshape_squeeze.3.index_from, s32[64,128]{1,0:T(8,128)S(1)} %bitcast.16, f32[4096,32]{1,0:T(8,128)S(1)} %copy.12.table_ref, s32[1]{0:T(128)} %bitcast.3.core_ref), custom_call_target="tpu_custom_call" | custom-call | tf_op jit(solution)/shard_map/answers/pallas_call | solution.py:132
  27.6 14.9 %all_to_all.30.part_ref = f32[32,16,128]{2,1,0:T(8,128)S(1)} all-to-all(f32[32,16,128]{2,1,0:T(8,128)S(1)} %answers.1), channel_id=1, replica_groups=mesh['y'=8,'x'=4,'z'=12,'core'=2] {'y','x'}, dimensions={0} | all-to-all | bytes 524288 | tf_op jit(solution)/shard_map/all_to_all | solution.py:28
  42.5 0.0 copy-done.1
  42.5 0.0 copy-done.2
  42.5 0.0 copy-done.3
  42.5 0.4 project.1
  42.9 2.1 %all_gather.6 = f32[2,2,24,1024]{3,2,1,0:T(8,128)S(1)} all-gather(f32[1,2,24,1024]{3,2,1,0:T(8,128)S(1)} %bitcast.17), channel_id=1, replica_groups=mesh['y'=8,'x'=4,'z'=12,'core'=2] {'core'}, dimensions={0}, use_global_device_ids=true | all-gather | bytes 589824 | tf_op jit(solution)/shard_map/all_gather | solution.py:256
  45.0 23.9 %all_to_all.31 = f32[12,8,256]{2,1,0:T(8,128)S(1)} all-to-all(f32[12,8,256]{2,1,0:T(8,128)S(1)} %bitcast.20), channel_id=1, replica_groups=mesh['y'=8,'x'=4,'z'=12,'core'=2] {'z'}, dimensions={0} | all-to-all | bytes 196608 | tf_op jit(solution)/shard_map/all_to_all | solution.py:28
  69.0 14.3 %all_to_all.32 = f32[12,8,256]{2,1,0:T(8,128)S(1)} all-to-all(f32[12,8,256]{2,1,0:T(8,128)S(1)} %broadcast_in_dim.4), channel_id=1, replica_groups=mesh['y'=8,'x'=4,'z'=12,'core'=2] {'z'}, dimensions={0} | all-to-all | bytes 196608 | tf_op jit(solution)/shard_map/all_to_all | solution.py:28
  83.2 1.9 %all_gather.7.pre_ref = f32[48,1024]{1,0:T(8,128)S(1)} all-gather(f32[24,1024]{1,0:T(8,128)S(1)} %bitcast.21), channel_id=1, replica_groups=mesh['y'=8,'x'=4,'z'=12,'core'=2] {'core'}, dimensions={0}, use_global_device_ids=true | all-gather | bytes 294912 | tf_op jit(solution)/shard_map/all_gather | solution.py:262
  85.2 0.0 copy-done
  85.2 0.9 gradients.1
  86.0 16.9 %all_to_all.33 = f32[32,16,128]{2,1,0:T(8,128)S(1)} all-to-all(f32[32,16,128]{2,1,0:T(8,128)S(1)} %get-tuple-element.12), channel_id=1, replica_groups=mesh['y'=8,'x'=4,'z'=12,'core'=2] {'y','x'}, dimensions={0} | all-to-all | bytes 524288 | tf_op jit(solution)/shard_map/all_to_all | solution.py:28
  103.0 15.9 %all_to_all.34.block_ref = f32[32,16,128]{2,1,0:T(8,128)S(1)} all-to-all(f32[32,16,128]{2,1,0:T(8,128)S(1)} %broadcast_in_dim.5), channel_id=1, replica_groups=mesh['y'=8,'x'=4,'z'=12,'core'=2] {'y','x'}, dimensions={0} | all-to-all | bytes 524288 | tf_op jit(solution)/shard_map/all_to_all | solution.py:28
  118.9 0.7 spread.1
  (6 shorter events, 0.1 us)
Async XLA Ops:
  2.6 21.8 %all-to-all-start = ((s32[32,2,128]{2,1,0:T(2,128)}), s32[32,2,128]{2,1,0:T(2,128)S(1)}, u32[]{:S(2)}, u32[]{:S(2)}) async-start(s32[32,2,128]{2,1,0:T(2,128)} %bitcast.22), calls=%async_computation | async-start | bytes 65536 | tf_op jit(solution)/shard_map/all_to_all | solution.py:28
  17.3 25.2 %copy-start.1 = (f32[32,1024]{1,0:T(8,128)S(1)}, f32[32,1024]{1,0:T(8,128)}, u32[]{:S(2)}) copy-start(f32[32,1024]{1,0:T(8,128)} %self_ref.1) | copy-start | bytes 393220
  17.3 25.2 %copy-start.2 = (f32[32,1024]{1,0:T(8,128)S(1)}, f32[32,1024]{1,0:T(8,128)}, u32[]{:S(2)}) copy-start(f32[32,1024]{1,0:T(8,128)} %neigh_ref.1) | copy-start | bytes 393220
  17.3 25.2 %copy-start.3 = (f32[48,32]{0,1:T(8,128)S(1)}, f32[48,32]{0,1:T(8,128)}, u32[]{:S(2)}) copy-start(f32[48,32]{0,1:T(8,128)} %param.8) | copy-start | bytes 18436
  24.5 60.6 %copy-start = (f32[48,1024]{1,0:T(8,128)S(1)}, f32[48,1024]{1,0:T(8,128)}, u32[]{:S(2)}) copy-start(f32[48,1024]{1,0:T(8,128)} %grad_ref.1) | copy-start | bytes 589828
